TPU v7x, 128 devices: a whole 4x4x4 slice. The times are simulated.
128 devices in a mesh: pp: 4 (over x_lo, core), ep: 32 (over z, x_hi, y).
Axes of the slice: x: 4 (x_hi: 2, x_lo: 2; x = x_hi * 2 + x_lo), y: 4, z: 4, core: 2. Of those that a mesh axis runs over, the one named last changes fastest.
Arguments:
- layer_input: bfloat16 [4, 4096, 2048], P('pp', 'ep'), may hold values from -6 to 6
- out_grad: bfloat16 [4, 4096, 2048], P('pp', 'ep'), may hold values from -1.5 to 1.5
- expert_ids: int32 [4, 4096, 8], P('pp', 'ep'), may hold values from 0 to 63, all different within a row; in each aligned block of 128 rows (0 to 127, 128 to 255, ..., all dimensions but the last counted through in order) at most 24 rows name the same one
- combine: float32 [4, 4096, 8], P('pp', 'ep'), may hold values from 0.05 to 1
- w_gate: bfloat16 [4, 64, 2048, 768], P('pp', 'ep'), may hold values from -0.125 to 0.125
- w_up: bfloat16 [4, 64, 2048, 768], P('pp', 'ep'), may hold values from -0.125 to 0.125
- w_down: bfloat16 [4, 64, 768, 2048], P('pp', 'ep'), may hold values from -0.21875 to 0.21875
Outputs:
- sent_grad: bfloat16 [4, 4096, 2048], P('pp', 'ep')
- combine_grad: bfloat16 [4, 4096, 8], P('pp', 'ep')
Inputs may be any that keep to these rules, and one draw needn't show every extreme that they name: `expert_ids`: the 8 ids of a token differ. Within the rows of one device no expert is named more than 24 times, and in some device's rows some expert is named exactly 24 times.
All inputs are finite; a program needn't handle non-finite values.
Results may differ from a plain program's by a relative error of at most 0.011.
Values may be sent and summed in bfloat16 or wider, within the bound.
A program may use at most 128 MiB of HBM per device.

v0:
```python
import jax
import jax.numpy as jnp
from jax import lax
from jax.sharding import PartitionSpec as P


def shifted(value, axis, steps):
    count = lax.axis_size(axis)
    pairs = [(source, (source + steps) % count) for source in range(count)]
    return lax.ppermute(value, axis, pairs)


def slot_table(ids_block, experts, capacity):
    flat = ids_block.reshape(-1)
    onehot = (flat[:, None] == jnp.arange(experts, dtype=jnp.int32)[None, :]).astype(jnp.int32)
    ranks = jnp.sum(jnp.cumsum(onehot, axis=0) * onehot, axis=1) - 1
    return flat * capacity + ranks


def dispatch(rows, slots, total_slots, choices):
    count = slots.shape[0]
    source = jnp.full((total_slots,), rows.shape[0], jnp.int32)
    source = source.at[slots].set(jnp.arange(count, dtype=jnp.int32) // choices)
    padded = jnp.concatenate([rows, jnp.zeros((1, rows.shape[1]), rows.dtype)], axis=0)
    return padded[source]


def expert_work(rows_in, grads_in, gate_w, up_w, down_w):
    gate_pre = jnp.einsum("secd,edf->secf", rows_in, gate_w, preferred_element_type=jnp.float32)
    up_value = jnp.einsum("secd,edf->secf", rows_in, up_w, preferred_element_type=jnp.float32)
    sigma = jax.nn.sigmoid(gate_pre)
    active = gate_pre * sigma
    hidden = (active * up_value).astype(jnp.bfloat16)
    expert_out = jnp.einsum("secf,efd->secd", hidden, down_w, preferred_element_type=jnp.float32)
    score = jnp.sum(expert_out * grads_in.astype(jnp.float32), axis=-1).astype(jnp.bfloat16)
    hidden_grad = jnp.einsum("secd,efd->secf", grads_in, down_w, preferred_element_type=jnp.float32)
    gate_grad = (hidden_grad * up_value * sigma * (1.0 + gate_pre * (1.0 - sigma))).astype(
        jnp.bfloat16
    )
    up_grad = (hidden_grad * active).astype(jnp.bfloat16)
    row_grad = jnp.einsum("secf,edf->secd", gate_grad, gate_w, preferred_element_type=jnp.float32)
    row_grad = row_grad + jnp.einsum(
        "secf,edf->secd", up_grad, up_w, preferred_element_type=jnp.float32
    )
    return (row_grad.astype(jnp.bfloat16), score)


def on_device(layer_input, out_grad, expert_ids, combine, w_gate, w_up, w_down):
    ranks_ep = lax.axis_size("ep")
    tok_count = layer_input.shape[1]
    width = layer_input.shape[2]
    choices = expert_ids.shape[2]
    per_device = w_gate.shape[1]
    experts = per_device * ranks_ep
    capacity = 3 * tok_count * choices // (2 * experts)
    slots = slot_table(expert_ids[0], experts, capacity)
    send_rows = dispatch(layer_input[0], slots, experts * capacity, choices)
    send_rows = send_rows.reshape(ranks_ep, per_device, capacity, width)
    send_grads = dispatch(out_grad[0], slots, experts * capacity, choices)
    send_grads = send_grads.reshape(ranks_ep, per_device, capacity, width)
    gate_w = w_gate[0]
    up_w = w_up[0]
    down_w = w_down[0]
    arrived = (
        lax.all_to_all(send_rows, "ep", split_axis=0, concat_axis=0, tiled=True),
        lax.all_to_all(send_grads, "ep", split_axis=0, concat_axis=0, tiled=True),
    )
    row_grad, score = expert_work(arrived[0], arrived[1], gate_w, up_w, down_w)
    back_rows, back_scores = (
        lax.all_to_all(row_grad, "ep", split_axis=0, concat_axis=0, tiled=True),
        lax.all_to_all(score, "ep", split_axis=0, concat_axis=0, tiled=True),
    )
    back_rows = back_rows.reshape(experts * capacity, width)
    back_scores = back_scores.reshape(experts * capacity)
    picked = back_rows[slots].reshape(tok_count, choices, width)
    input_grad = jnp.einsum("tk,tkd->td", combine[0], picked.astype(jnp.float32)).astype(
        jnp.bfloat16
    )
    scores = back_scores[slots].reshape(tok_count, choices)
    sent_grad = shifted(input_grad[None], "pp", -1)
    return (sent_grad, scores[None])


def solution(mesh):
    return jax.shard_map(
        on_device,
        mesh=mesh,
        in_specs=(
            P("pp", "ep", None),
            P("pp", "ep", None),
            P("pp", "ep", None),
            P("pp", "ep", None),
            P("pp", "ep", None, None),
            P("pp", "ep", None, None),
            P("pp", "ep", None, None),
        ),
        out_specs=(P("pp", "ep", None), P("pp", "ep", None)),
        check_vma=False,
    )
```

profile of v0, /device:TPU:0, one launch (start us, length us, event | category | flops | bytes accessed | tf_op | source)
XLA Modules:
  0.0 430.3 jit_solution(6839027605216994812)
XLA Ops:
  0.6 0.7 broadcast_multiply_fusion
  1.3 0.8 copy.43
  2.1 0.1 eq.29
  2.2 0.1 eq.25
  2.3 0.1 copy.42
  2.4 0.1 mul.45
  2.5 18.0 %reduce-window.6 = s32[64,8,128]{2,1,0:T(8,128)S(1)} reduce-window(s32[64,8,128]{2,1,0:T(8,128)S(1)} %fusion.39, s32[]{:T(128)} %constant.34.clone.1), window={size=1x1x128 pad=0_0x0_0x127_0}, to_apply=%region_0.0 | reduce-window | flops 8323072 | bytes 524292 | tf_op jit(solution)/shard_map/reduce-window
  20.5 0.1 slice.16
  20.7 0.1 copy.45
  20.9 0.1 copy.46
  20.9 0.1 broadcast_add_fusion
  21.1 0.1 fusion.38
  21.2 4.3 %scatter_custom_fusion = s32[1536]{0:T(1024)S(1)} fusion(s32[1024]{0:T(1024)S(1)} %bitcast.122, s32[1024]{0:T(1024)S(1)} %add_select_fusion, s32[]{:T(128)} %constant.32.clone.1), kind=kCustom, calls=%fused_computation.60 | custom fusion | bytes 6148 | tf_op jit(solution)/shard_map/scatter | solution.py:23
  25.5 1.1 concatenate.7
  26.6 7.1 %gather_fusion.1 = bf16[1536,2048]{1,0:T(8,128)(2,1)} fusion(bf16[129,2048]{1,0:T(8,128)(2,1)S(1)} %concatenate.7, s32[2048]{0:T(1024)S(1)} %pad_clamp_fusion), kind=kCustom, calls=%fused_computation.1 | custom fusion | bytes 12589056 | tf_op jit(solution)/shard_map/gather | solution.py:25
  33.8 0.0 copy-start
  33.8 11.1 %all-to-all-start.1 = ((bf16[32,2,24,2048]{3,2,1,0:T(8,128)(2,1)}), bf16[32,2,24,2048]{3,2,1,0:T(8,128)(2,1)}, u32[]{:S(2)}, u32[]{:S(2)}) async-start(bf16[32,2,24,2048]{3,2,1,0:T(8,128)(2,1)} %bitcast.116), calls=%async_computation.1 | async-start | bytes 12582912 | tf_op jit(solution)/shard_map/all_to_all | solution.py:65
  44.9 0.0 copy-done
  45.0 7.1 %gather_fusion = bf16[1536,2048]{1,0:T(8,128)(2,1)} fusion(bf16[129,2048]{1,0:T(8,128)(2,1)S(1)} %concatenate.6, s32[2048]{0:T(1024)S(1)} %pad_clamp_fusion), kind=kCustom, calls=%fused_computation | custom fusion | bytes 12589056 | tf_op jit(solution)/shard_map/gather | solution.py:25
  52.1 82.4 %all-to-all-done.1 = bf16[32,2,24,2048]{3,2,1,0:T(8,128)(2,1)} async-done(((bf16[32,2,24,2048]{3,2,1,0:T(8,128)(2,1)}), bf16[32,2,24,2048]{3,2,1,0:T(8,128)(2,1)}, u32[]{:S(2)}, u32[]{:S(2)}) %all-to-all-start.1) | async-done | bytes 6291488 | tf_op jit(solution)/shard_map/all_to_all | solution.py:65
  134.5 7.4 %all-to-all-start = ((bf16[32,2,24,2048]{3,2,1,0:T(8,128)(2,1)}), bf16[32,2,24,2048]{3,2,1,0:T(8,128)(2,1)}, u32[]{:S(2)}, u32[]{:S(2)}) async-start(bf16[32,2,24,2048]{3,2,1,0:T(8,128)(2,1)} %bitcast.115), calls=%async_computation | async-start | bytes 12582912 | tf_op jit(solution)/shard_map/all_to_all | solution.py:66
  141.9 10.4 %fusion.4 = f32[2,32,24,768]{3,2,1,0:T(8,128)} fusion(bf16[1,2,2048,768]{3,2,1,0:T(8,128)(2,1)} %param.11, bf16[32,2,24,2048]{3,2,1,0:T(8,128)(2,1)} %all-to-all-done.1), kind=kOutput, calls=%fused_computation.11 | convolution fusion | flops 4831838208 | bytes 17301504 | tf_op jit(solution)/shard_map/secd,edf->secf/dot_general | solution.py:29
  152.3 10.4 %fusion.12 = f32[2,32,24,768]{3,2,1,0:T(8,128)} fusion(bf16[1,2,2048,768]{3,2,1,0:T(8,128)(2,1)} %param.12, bf16[32,2,24,2048]{3,2,1,0:T(8,128)(2,1)} %all-to-all-done.1), kind=kOutput, calls=%fused_computation.19 | convolution fusion | flops 4831838208 | bytes 17301504 | tf_op jit(solution)/shard_map/secd,edf->secf/dot_general | solution.py:30
  162.7 62.7 %all-to-all-done = bf16[32,2,24,2048]{3,2,1,0:T(8,128)(2,1)} async-done(((bf16[32,2,24,2048]{3,2,1,0:T(8,128)(2,1)}), bf16[32,2,24,2048]{3,2,1,0:T(8,128)(2,1)}, u32[]{:S(2)}, u32[]{:S(2)}) %all-to-all-start) | async-done | bytes 6291488 | tf_op jit(solution)/shard_map/all_to_all | solution.py:66
  225.4 0.0 copy-start.2
  225.4 10.6 %fusion.8 = f32[2,32,24,768]{3,2,1,0:T(8,128)} fusion(bf16[1,2,768,2048]{3,2,1,0:T(8,128)(2,1)} %param.13, bf16[32,2,24,2048]{3,2,1,0:T(8,128)(2,1)} %all-to-all-done), kind=kOutput, calls=%fused_computation.15 | convolution fusion | flops 4831838208 | bytes 17301504 | tf_op jit(solution)/shard_map/secd,efd->secf/dot_general | solution.py:36
  236.0 0.0 copy-done.2
  236.0 13.3 %fusion.2 = f32[2,32,24,2048]{3,2,1,0:T(8,128)} fusion(bf16[1,2,2048,768]{3,2,1,0:T(8,128)(2,1)} %param.11, f32[2,32,24,768]{3,2,1,0:T(8,128)S(1)} %copy-done.2, f32[2,32,24,768]{3,2,1,0:T(8,128)} %fusion.12, f32[2,32,24,768]{3,2,1,0:T(8,128)} %fusion.8), kind=kOutput, calls=%fused_computation.9 | convolution fusion | flops 4843634688 | bytes 33030144 | tf_op jit(solution)/shard_map/secf,edf->secd/dot_general | solution.py:41
  249.3 14.1 %fusion.1 = bf16[32,2,24,2048]{3,2,0,1:T(8,128)(2,1)} fusion(f32[2,32,24,2048]{3,2,1,0:T(8,128)} %fusion.2, bf16[1,2,2048,768]{3,2,1,0:T(8,128)(2,1)} %param.12, f32[2,32,24,768]{3,2,1,0:T(8,128)} %fusion.8, f32[2,32,24,768]{3,2,1,0:T(8,128)} %fusion.4), kind=kOutput, calls=%fused_computation.8 | convolution fusion | flops 4845207552 | bytes 34603008 | tf_op jit(solution)/shard_map/secf,edf->secd/dot_general | solution.py:42
  263.4 6.6 %copy.50 = bf16[32,2,24,2048]{3,2,1,0:T(8,128)(2,1)} copy(bf16[32,2,24,2048]{3,2,0,1:T(8,128)(2,1)} %fusion.1) | data formatting | bytes 12582912 | tf_op jit(solution)/shard_map/convert_element_type | solution.py:45
  270.0 0.0 copy-start.1
  270.0 7.2 %all-to-all-start.2 = ((bf16[32,2,24,2048]{3,2,1,0:T(8,128)(2,1)}), bf16[32,2,24,2048]{3,2,1,0:T(8,128)(2,1)}, u32[]{:S(2)}, u32[]{:S(2)}) async-start(bf16[32,2,24,2048]{3,2,1,0:T(8,128)(2,1)} %copy.50), calls=%async_computation.2 | async-start | bytes 12582912 | tf_op jit(solution)/shard_map/all_to_all | solution.py:70
  277.1 0.0 copy-done.1
  277.1 0.1 copy.58
  277.3 82.9 %all-to-all-done.2 = bf16[32,2,24,2048]{3,2,1,0:T(8,128)(2,1)} async-done(((bf16[32,2,24,2048]{3,2,1,0:T(8,128)(2,1)}), bf16[32,2,24,2048]{3,2,1,0:T(8,128)(2,1)}, u32[]{:S(2)}, u32[]{:S(2)}) %all-to-all-start.2) | async-done | bytes 6291488 | tf_op jit(solution)/shard_map/all_to_all | solution.py:70
  360.2 12.4 %gather_fusion.2 = bf16[1024,2048]{1,0:T(8,128)(2,1)} fusion(bf16[1536,2048]{1,0:T(8,128)(2,1)} %bitcast.22, s32[1024]{0:T(1024)S(1)} %broadcast_clamp_fusion), kind=kCustom, calls=%fused_computation.2 | custom fusion | bytes 8392704 | tf_op jit(solution)/shard_map/gather | solution.py:75
  372.6 3.4 fusion.28
  376.0 0.3 copy.72
  376.3 5.1 %collective-permute-start = (bf16[1,128,2048]{2,1,0:T(8,128)(2,1)S(1)}, bf16[1,128,2048]{2,1,0:T(8,128)(2,1)S(1)}, u32[]{:S(2)}, u32[]{:S(2)}) collective-permute-start(bf16[1,128,2048]{2,1,0:T(8,128)(2,1)S(1)} %bitcast.118), channel_id=1, source_target_pairs={{0,96},{32,0},{64,32},{96,64},{1,97},{33,1},{65,33},{97,65},{2,98}... | collective-permute-start | bytes 1572872 | tf_op jit(solution)/shard_map/ppermute | solution.py:10
  381.4 11.0 %fusion = bf16[32,2,24]{2,0,1:T(8,128)(2,1)S(1)} fusion(bf16[32,2,24,2048]{3,2,1,0:T(8,128)(2,1)} %all-to-all-done, bf16[1,2,768,2048]{3,2,1,0:T(8,128)(2,1)} %param.13, f32[2,32,24,768]{3,2,1,0:T(8,128)} %fusion.12, f32[2,32,24,768]{3,2,1,0:T(8,128)} %fusion.4), kind=kOutput, calls=%fused_computation.6 | convolution fusion | flops 4848351744 | bytes 22023168 | tf_op jit(solution)/shard_map/secf,efd->secd/dot_general | solution.py:34
  392.5 0.1 copy.52
  392.5 0.1 copy.53
  392.6 29.2 %all_to_all.20 = bf16[32,2,24]{2,1,0:T(2,128)(2,1)S(1)} all-to-all(bf16[32,2,24]{2,1,0:T(2,128)(2,1)S(1)} %copy.53), channel_id=1, replica_groups=mesh['pp'=4,'ep'=32] {'ep'}, dimensions={0} | all-to-all | bytes 6144 | tf_op jit(solution)/shard_map/all_to_all | solution.py:71
  421.9 0.1 reshape.74
  422.0 6.8 %gather_fusion.3 = bf16[1024]{0:T(1024)(128)(2,1)S(1)} fusion(bf16[1536]{0:T(1024)(128)(2,1)S(1)} %reshape.74, s32[1024]{0:T(1024)S(1)} %broadcast_clamp_fusion), kind=kCustom, calls=%fused_computation.3 | custom fusion | bytes 8192 | tf_op jit(solution)/shard_map/gather | solution.py:79
  428.8 0.1 broadcast_in_dim_reshape.3
  428.9 0.7 copy.54
  429.5 0.0 collective-permute-done
  429.6 0.8 copy.74
  (10 shorter events, 0.1 us)
Async XLA Ops:
  33.8 11.1 %copy-start = (bf16[1,128,2048]{2,1,0:T(8,128)(2,1)S(1)}, bf16[1,128,2048]{2,1,0:T(8,128)(2,1)}, u32[]{:S(2)}) copy-start(bf16[1,128,2048]{2,1,0:T(8,128)(2,1)} %param.8) | copy-start | bytes 1572868
  33.8 100.7 %all-to-all-start.1 = ((bf16[32,2,24,2048]{3,2,1,0:T(8,128)(2,1)}), bf16[32,2,24,2048]{3,2,1,0:T(8,128)(2,1)}, u32[]{:S(2)}, u32[]{:S(2)}) async-start(bf16[32,2,24,2048]{3,2,1,0:T(8,128)(2,1)} %bitcast.116), calls=%async_computation.1 | async-start | bytes 12582912 | tf_op jit(solution)/shard_map/all_to_all | solution.py:65
  134.5 90.9 %all-to-all-start = ((bf16[32,2,24,2048]{3,2,1,0:T(8,128)(2,1)}), bf16[32,2,24,2048]{3,2,1,0:T(8,128)(2,1)}, u32[]{:S(2)}, u32[]{:S(2)}) async-start(bf16[32,2,24,2048]{3,2,1,0:T(8,128)(2,1)} %bitcast.115), calls=%async_computation | async-start | bytes 12582912 | tf_op jit(solution)/shard_map/all_to_all | solution.py:66
  225.4 10.6 %copy-start.2 = (f32[2,32,24,768]{3,2,1,0:T(8,128)S(1)}, f32[2,32,24,768]{3,2,1,0:T(8,128)}, u32[]{:S(2)}) copy-start(f32[2,32,24,768]{3,2,1,0:T(8,128)} %fusion.4) | copy-start | bytes 14155780
  270.0 7.2 %copy-start.1 = (f32[1,128,8]{1,2,0:T(8,128)S(1)}, f32[1,128,8]{1,2,0:T(8,128)}, u32[]{:S(2)}) copy-start(f32[1,128,8]{1,2,0:T(8,128)} %param.10) | copy-start | bytes 12292
  270.0 90.2 %all-to-all-start.2 = ((bf16[32,2,24,2048]{3,2,1,0:T(8,128)(2,1)}), bf16[32,2,24,2048]{3,2,1,0:T(8,128)(2,1)}, u32[]{:S(2)}, u32[]{:S(2)}) async-start(bf16[32,2,24,2048]{3,2,1,0:T(8,128)(2,1)} %copy.50), calls=%async_computation.2 | async-start | bytes 12582912 | tf_op jit(solution)/shard_map/all_to_all | solution.py:70
  376.3 53.2 %collective-permute-start = (bf16[1,128,2048]{2,1,0:T(8,128)(2,1)S(1)}, bf16[1,128,2048]{2,1,0:T(8,128)(2,1)S(1)}, u32[]{:S(2)}, u32[]{:S(2)}) collective-permute-start(bf16[1,128,2048]{2,1,0:T(8,128)(2,1)S(1)} %bitcast.118), channel_id=1, source_target_pairs={{0,96},{32,0},{64,32},{96,64},{1,97},{33,1},{65,33},{97,65},{2,98}... | collective-permute-start | bytes 1572872 | tf_op jit(solution)/shard_map/ppermute | solution.py:10
where the time goes:
time: 431 us; the launch traced here: 430 us
  waiting for transfers between devices  228 us (53%)
  matrix products  73.2 us (17%)
  local copies, waits for them, and re-layouts  49.3 us (11%)
  starting transfers between devices  30.8 us (7%)
  blocking collectives  29.2 us (7%)
  other arithmetic  19 us (4%)
    all_to_all x1, waiting for transfers between devices, on_device(): lax.all_to_all(row_grad, 'ep', split_axis=0, concat_axis=0, tiled=True)  82.9 us
    all_to_all x1, waiting for transfers between devices, on_device(): lax.all_to_all(send_rows, 'ep', split_axis=0, concat_axis=0, tiled=True)  82.4 us
    all_to_all x1, waiting for transfers between devices, on_device(): lax.all_to_all(send_grads, 'ep', split_axis=0, concat_axis=0, tiled=True)  62.7 us
    all_to_all x1, blocking collectives, on_device(): lax.all_to_all(score, 'ep', split_axis=0, concat_axis=0, tiled=True)  29.2 us
    another operation x3, other arithmetic  18.2 us
    gather x2, local copies, waits for them, and re-layouts, dispatch(): return padded[source]  14.2 us
    dot_general x1, matrix products, expert_work(): jnp.einsum('secf,edf->secd', up_grad, up_w, preferred_element_type=jnp.fl...  14.1 us
    dot_general x1, matrix products, expert_work(): jnp.einsum('secf,edf->secd', gate_grad, gate_w, preferred_element_type=jn...  13.3 us
  transfers between devices with their start and end apart: 4, of which 3 were waited for; matrix products, arithmetic and copies ran while one was open for 11% of the time, Pallas kernels for 0%

commit v1 on v0

v1 whole, which is shorter than its diff:
```python
import functools

import jax
import jax.numpy as jnp
from jax import lax
from jax.experimental import pallas as pl
from jax.experimental.pallas import tpu as pltpu
from jax.sharding import PartitionSpec as P

MESH = pl.DeviceIdType.MESH
LINE = 4
ORDER = (0, -1, 1, 2)
BF16 = jnp.bfloat16
F32 = jnp.float32
ROWS, GRADS = 0, 1


def kernel(
    tok, cap, width, hidden_units,
    rows_in, grads_in, meta_in, gate_w, up_w, down_w,
    out_ref, cg_ref,
    blocks, metas, staged, arrived, returned, near, far, final,
    sel_s, wsel_s, wg, wu, wd, gg_s, ug_s, score_s, score_acc, score_r, cg_s, cg_r,
    x_send, x_recv, ag_send, ag_recv, meta_send, meta_recv, own_sem, w_sem,
    fwd_send, fwd_recv, ret_send, ret_recv, ret_own, sc_send, sc_recv, cg_send, cg_recv,
    rs_send, rs_recv, fin_send, fin_recv,
):
    slot = 2 * cap
    group = LINE * slot
    half = tok // 2
    cols = width // 2
    pair = 2 * tok
    per_expert = LINE * group
    pp, ep = lax.axis_index("pp"), lax.axis_index("ep")
    z, xh, y = ep // 8, (ep // 4) % 2, ep % 4
    line, cross = (z, y), (y, z)
    inputs = (rows_in, grads_in)

    def wrap(v):
        return lax.rem(v + LINE, LINE)

    def device(p, line_at, x_at, cross_at, section=None):
        z_at, y_at = (line_at, cross_at) if p == ROWS else (cross_at, line_at)
        return {"pp": pp if section is None else section, "ep": z_at * 8 + x_at * 4 + y_at}

    def remote(src, dst, send, recv, to):
        return pltpu.make_async_remote_copy(
            src_ref=src, dst_ref=dst, send_sem=send, recv_sem=recv, device_id=to, device_id_type=MESH
        )

    def place(p, line_at, x_at, part=None):
        start = ((p * LINE + line_at) * 2 + x_at) * tok
        if part is None:
            return blocks.at[pl.ds(pl.multiple_of(start, tok), tok), :]
        return blocks.at[pl.ds(pl.multiple_of(start + part * half, half), half), :]

    before, after = lax.rem(pp + 3, 4), lax.rem(pp + 1, 4)
    peers = [device(ROWS, wrap(z + o), x_at, y) for o in ORDER for x_at in (xh, 1 - xh)][1:]
    peers += [device(GRADS, wrap(y + o), x_at, z) for o in ORDER[1:] for x_at in (xh, 1 - xh)]
    peers += [device(ROWS, z, x_at, y, s) for x_at in (xh, 1 - xh) for s in (before, after)]
    barrier = pltpu.get_barrier_semaphore()
    for peer in peers:
        pl.semaphore_signal(barrier, inc=1, device_id=peer, device_id_type=MESH)
    pl.semaphore_wait(barrier, len(peers))

    def x_copy(p, part):
        rows = pl.ds(part * half, half)
        return remote(
            inputs[p].at[rows, :], place(p, line[p], xh, part), x_send.at[p, part], x_recv.at[p, part],
            device(p, line[p], 1 - xh, cross[p]),
        )

    def x_wait(p, part):
        remote(
            inputs[p].at[pl.ds(part * half, half), :], place(p, line[p], 1 - xh, part),
            x_send.at[p, part], x_recv.at[p, part], device(p, line[p], 1 - xh, cross[p]),
        ).wait_recv()

    def ag_part(d, k):
        return (d + k) % 2 if k < 2 else d

    def ag_copy(p, q, d, k):
        step = 1 - 2 * d
        part = ag_part(d, k)
        x_at = xh if q == 0 else 1 - xh
        at = line[p] if k < 2 else wrap(line[p] - step)
        dst = place(p, at, x_at, part)
        src = inputs[p].at[pl.ds(part * half, half), :] if q == 0 and k < 2 else dst
        return remote(
            src, dst, ag_send.at[p, q, d, k], ag_recv.at[p, q, d, k],
            device(p, wrap(line[p] + step), xh, cross[p]),
        )

    def ag_wait(p, q, d, k):
        step = 1 - 2 * d
        x_at = xh if q == 0 else 1 - xh
        at = wrap(line[p] - step) if k < 2 else wrap(line[p] + 2)
        dst = place(p, at, x_at, ag_part(d, k))
        remote(
            dst, dst, ag_send.at[p, q, d, k], ag_recv.at[p, q, d, k],
            device(p, wrap(line[p] + step), xh, cross[p]),
        ).wait_recv()

    def meta_copy(p, i, q):
        return remote(
            meta_in, metas.at[p, line[p], xh], meta_send.at[p, i, q], meta_recv.at[p, i, q],
            device(p, wrap(line[p] + ORDER[i]), xh if q == 0 else 1 - xh, cross[p]),
        )

    def meta_wait(p, i, q):
        remote(
            meta_in, metas.at[p, wrap(line[p] - ORDER[i]), xh if q == 0 else 1 - xh],
            meta_send.at[p, i, q], meta_recv.at[p, i, q],
            device(p, wrap(line[p] + ORDER[i]), xh if q == 0 else 1 - xh, cross[p]),
        ).wait_recv()

    others = [(i, q) for i in range(LINE) for q in range(2) if (i, q) != (0, 0)]
    paths = (ROWS, GRADS)
    for p in paths:
        for i, q in others:
            meta_copy(p, i, q).start()
    for p in paths:
        for part in range(2):
            x_copy(p, part).start()
    for k in range(2):
        for p in paths:
            for d in range(2):
                ag_copy(p, 0, d, k).start()
    own = []
    for p in paths:
        own.append(pltpu.make_async_copy(inputs[p], place(p, line[p], xh), own_sem.at[p]))
        own[-1].start()
        metas[p, line[p], xh] = meta_in[...]

    def weights(e):
        return [
            pltpu.make_async_copy(src.at[e], dst, w_sem.at[i])
            for i, (src, dst) in enumerate(((gate_w, wg), (up_w, wu), (down_w, wd)))
        ]

    for copy in weights(0):
        copy.start()
    for p in paths:
        for i, q in others:
            meta_wait(p, i, q)

    def expert_numbers(p):
        row = lax.broadcasted_iota(jnp.int32, (8, tok), 0)
        e, across = row // LINE, (row + cross[p]) % LINE
        if p == ROWS:
            return 16 * z + 8 * xh + 2 * across + e
        return 16 * across + 8 * xh + 2 * y + e

    earlier = (
        lax.broadcasted_iota(jnp.int32, (tok, tok), 0) < lax.broadcasted_iota(jnp.int32, (tok, tok), 1)
    ).astype(F32).astype(BF16)
    rank_no = lax.broadcasted_iota(jnp.int32, (cap, tok), 0).astype(F32)
    nothing = jnp.zeros((cap, tok), F32)

    for p in paths:
        numbers = expert_numbers(p).astype(F32)

        def build(i, carry, p=p, numbers=numbers):
            at = wrap(line[p] + jnp.where(i == 0, 0, jnp.where(i == 1, -1, i - 1)))
            found, weight, rank = [], [], []
            for h in range(2):
                meta = metas[p, at, h]
                member = jnp.zeros((8, tok), F32)
                share = jnp.zeros((8, tok), F32)
                for k in range(8):
                    same = meta[k : k + 1, :] == numbers
                    member = member + jnp.where(same, 1.0, 0.0)
                    share = share + jnp.where(same, meta[8 + k : 9 + k, :], 0.0)
                before_it = jnp.dot(member.astype(BF16), earlier, preferred_element_type=F32)
                rank.append(jnp.where(member > 0.0, before_it, -1.0))
                weight.append(share)
            hot, hot_w = [], []
            for row in range(8):
                for h in range(2):
                    hit = rank[h][row : row + 1, :] == rank_no
                    one = jnp.where(hit, 1.0, 0.0)
                    scaled = jnp.where(hit, weight[h][row : row + 1, :], 0.0)
                    hot.append(jnp.concatenate([one, nothing] if h == 0 else [nothing, one], axis=1))
                    hot_w.append(jnp.concatenate([scaled, nothing] if h == 0 else [nothing, scaled], axis=1))
            sel_s[p, i] = jnp.concatenate(hot, axis=0).astype(BF16)
            wsel_s[p, i] = jnp.concatenate(hot_w, axis=0).T.astype(BF16)
            return carry

        lax.fori_loop(0, LINE, build, 0)

    def arrived_at(p, e, from_cross, at):
        y_src, z_src = (from_cross, at) if p == ROWS else (at, from_cross)
        start = ((y_src * LINE) + z_src) * slot + (p * 2 + e) * per_expert
        return arrived.at[pl.ds(pl.multiple_of(start, 16), slot), :]

    def fwd_copy(p, e, j, i):
        at = wrap(line[p] + ORDER[i])
        return remote(
            staged.at[pl.ds((((p * 3 + j - 1) * 2 + e) * LINE + i) * slot, slot), :],
            arrived_at(p, e, cross[p], at), fwd_send.at[p, e, j - 1, i], fwd_recv.at[p, e, j - 1, i],
            device(p, line[p], xh, wrap(cross[p] + j)),
        )

    def fwd_wait(p, e, j, i):
        dst = arrived_at(p, e, wrap(cross[p] - j), wrap(line[p] + ORDER[i]))
        remote(
            dst, dst, fwd_send.at[p, e, j - 1, i], fwd_recv.at[p, e, j - 1, i],
            device(p, line[p], xh, wrap(cross[p] + j)),
        ).wait_recv()

    tile = 512

    def select(p, i):
        at = wrap(line[p] + ORDER[i])
        start = pl.multiple_of((p * LINE + at) * pair, pair)

        @pl.loop(0, width // tile)
        def _(n):
            lanes = pl.ds(pl.multiple_of(n * tile, tile), tile)
            picked = jnp.dot(
                sel_s[p, i], blocks[pl.ds(start, pair), lanes], preferred_element_type=F32
            ).astype(BF16)
            for e in range(2):
                for j in range(LINE):
                    part = picked[(e * LINE + j) * slot : (e * LINE + j + 1) * slot]
                    if j == 0:
                        arrived_at(p, e, cross[p], at)[:, lanes] = part
                    else:
                        first = (((p * 3 + j - 1) * 2 + e) * LINE + i) * slot
                        staged[pl.ds(first, slot), lanes] = part

    far_first = (2, 1, 3)

    def send_selected(e, i):
        for j in far_first:
            for p in paths:
                fwd_copy(p, e, j, i).start()

    for p in paths:
        for d in range(2):
            ag_wait(p, 0, d, 0)
            ag_copy(p, 0, d, 2).start()
    for part in range(2):
        for p in paths:
            x_wait(p, part)
            ag_copy(p, 1, part, 0).start()
    for p in paths:
        for d in range(2):
            ag_copy(p, 1, d, 1).start()
    for p in paths:
        own[p].wait()
        select(p, 0)
    send_selected(0, 0)
    for p in paths:
        for d in range(2):
            ag_wait(p, 1, d, 0)
            ag_copy(p, 1, d, 2).start()
    for i in (1, 2):
        for p in paths:
            for q in range(2):
                ag_wait(p, q, i - 1, 1)
            select(p, i)
        send_selected(0, i)
    for p in paths:
        for q in range(2):
            for d in range(2):
                ag_wait(p, q, d, 2)
        select(p, 3)
    send_selected(0, 3)
    for i in range(LINE):
        send_selected(1, i)
    for p in paths:
        for part in range(2):
            x_copy(p, part).wait_send()
        for q in range(2):
            for d in range(2):
                for k in range(3):
                    ag_copy(p, q, d, k).wait_send()
        for i, q in others:
            meta_copy(p, i, q).wait_send()

    def grad_rows(p, e, j):
        start = e * per_expert + wrap(cross[p] + j) * group
        return blocks.at[pl.ds(pl.multiple_of(start, 16), group), pl.ds(p * cols, cols)]

    def ret_copy(p, e, j):
        return remote(
            grad_rows(p, e, j), returned.at[p, e, LINE - j], ret_send.at[p, e, j - 1], ret_recv.at[p, e, j - 1],
            device(p, line[p], xh, wrap(cross[p] + j)),
        )

    def ret_wait(p, e, j):
        dst = returned.at[p, e, LINE - j]
        remote(
            dst, dst, ret_send.at[p, e, j - 1], ret_recv.at[p, e, j - 1],
            device(p, line[p], xh, wrap(cross[p] + j)),
        ).wait_recv()

    def own_return(p, e):
        return pltpu.make_async_copy(grad_rows(p, e, 0), returned.at[p, e, 0], ret_own.at[p, e])

    transposed = (((1,), (1,)), ((), ()))
    f_tile = 256
    d_tile = 256
    low = lax.broadcasted_iota(jnp.int32, (per_expert, 128), 1) < 64

    def expert(e):
        for copy in weights(e):
            copy.wait()
        for i in range(LINE):
            for p in paths:
                for j in far_first:
                    fwd_wait(p, e, j, i)
        row_at = pl.ds(e * per_expert, per_expert)
        grad_at = pl.ds((2 + e) * per_expert, per_expert)

        @pl.loop(0, hidden_units // f_tile)
        def _(n):
            units = pl.ds(pl.multiple_of(n * f_tile, f_tile), f_tile)
            gate = jnp.dot(arrived[row_at, :], wg[:, units], preferred_element_type=F32)
            up = jnp.dot(arrived[row_at, :], wu[:, units], preferred_element_type=F32)
            back = lax.dot_general(arrived[grad_at, :], wd[units, :], transposed, preferred_element_type=F32)
            sigma = jax.nn.sigmoid(gate)
            active = gate * sigma
            hidden = (active * up).astype(BF16).astype(F32)
            term = hidden * back
            gg_s[:, units] = (back * up * sigma * (1.0 + gate * (1.0 - sigma))).astype(BF16)
            ug_s[:, units] = (back * active).astype(BF16)
            term = term[:, :128] + term[:, 128:]

            @pl.when(n == 0)
            def _():
                score_acc[...] = term

            @pl.when(n > 0)
            def _():
                score_acc[...] += term

        score = jnp.broadcast_to(jnp.sum(score_acc[...], axis=1, keepdims=True), (per_expert, 128))
        if e == 0:
            score_s[...] = score.astype(BF16)
        else:
            score_s[...] = jnp.where(low, score_s[...].astype(F32), score).astype(BF16)

        for p in paths:

            @pl.loop(0, cols // d_tile)
            def _(n, p=p):
                lanes = pl.ds(pl.multiple_of(p * cols + n * d_tile, d_tile), d_tile)
                grad = lax.dot_general(gg_s[...], wg[lanes, :], transposed, preferred_element_type=F32)
                grad = grad + lax.dot_general(ug_s[...], wu[lanes, :], transposed, preferred_element_type=F32)
                grad = grad.astype(BF16)
                if p == ROWS:
                    blocks[pl.ds(e * per_expert, per_expert), lanes] = grad
                else:
                    for y_src in range(LINE):
                        for z_src in range(LINE):
                            to = e * per_expert + (z_src * LINE + y_src) * slot
                            source = (y_src * LINE + z_src) * slot
                            blocks[pl.ds(to, slot), lanes] = grad[source : source + slot]

            for j in far_first:
                ret_copy(p, e, j).start()
            own_return(p, e).start()

    def score_rows(j):
        return score_s.at[pl.ds(pl.multiple_of(wrap(y + j) * group, 16), group), :]

    def score_copy(j):
        return remote(
            score_rows(j), score_r.at[LINE - j], sc_send.at[j - 1], sc_recv.at[j - 1],
            device(ROWS, z, xh, wrap(y + j)),
        )

    expert(0)
    for copy in weights(1):
        copy.start()
    expert(1)
    for j in far_first:
        score_copy(j).start()
    score_r[0] = score_rows(0)[...]
    for p in paths:
        for e in range(2):
            for j in far_first:
                for i in range(LINE):
                    fwd_copy(p, e, j, i).wait_send()

    def partial_at(p, at, x_at, part=None):
        start = (at * 2 + x_at) * tok
        lanes = pl.ds(p * cols, cols)
        if part is None:
            return staged.at[pl.ds(pl.multiple_of(start, tok), tok), lanes]
        return staged.at[pl.ds(pl.multiple_of(start + part * half, half), half), lanes]

    def combine(p, i):
        at = wrap(line[p] + ORDER[i])
        take = pl.ds(pl.multiple_of(at * slot, 16), slot)
        gathered = jnp.concatenate([returned[p, e, j, take, :] for e in range(2) for j in range(LINE)], axis=0)
        rows = pl.ds(pl.multiple_of(at * pair, pair), pair)
        for n in range(cols // tile):
            staged[rows, pl.ds(p * cols + n * tile, tile)] = jnp.dot(
                wsel_s[p, i], gathered[:, n * tile : (n + 1) * tile], preferred_element_type=F32
            ).astype(BF16)

    def rs_copy(p, q, d, k):
        step = 1 - 2 * d
        x_at = xh if q == 0 else 1 - xh
        at = wrap(line[p] + 2) if k == 0 else wrap(line[p] + step)
        part = 1 - d if k == 1 else d
        dst = far.at[p, q, d] if k == 0 else near.at[p, q, d, part]
        return remote(
            partial_at(p, at, x_at, part), dst, rs_send.at[p, q, d, k], rs_recv.at[p, q, d, k],
            device(p, wrap(line[p] + step), xh, cross[p]),
        )

    def fin_copy(p, q):
        x_at = xh if q == 0 else 1 - xh
        return remote(
            partial_at(p, line[p], x_at), final.at[q, p], fin_send.at[p, q], fin_recv.at[p, q],
            device(p, line[p], x_at, cross[p], before),
        )

    def cg_copy(i, q):
        return remote(
            cg_s.at[i, q], cg_r.at[i, q], cg_send.at[i, q], cg_recv.at[i, q],
            device(ROWS, wrap(z + ORDER[i]), xh if q == 0 else 1 - xh, y),
        )

    for p in paths:
        for e in range(2):
            for j in far_first:
                ret_wait(p, e, j)
            own_return(p, e).wait()
        combine(p, 3)
        for q in (1, 0):
            for d in range(2):
                rs_copy(p, q, d, 0).start()
        for i in (1, 2):
            combine(p, i)
            for q in (1, 0):
                rs_copy(p, q, 2 - i, 1).start()
        combine(p, 0)

    for j in far_first:
        score_copy(j).wait_recv()
    lane = lax.broadcasted_iota(jnp.int32, (slot, 128), 1)
    numbers = expert_numbers(ROWS).astype(F32)
    for i in range(LINE):
        at = wrap(z + ORDER[i])
        take = pl.ds(pl.multiple_of(at * slot, 16), slot)
        spread = []
        for e in range(2):
            for j in range(LINE):
                mine = (lane // 64 == e) & (lane % 8 == e * LINE + j)
                spread.append(jnp.where(mine, score_r[j, take, :].astype(F32), 0.0))
        spread = jnp.concatenate(spread, axis=0).T.astype(BF16)
        by_expert = jnp.dot(spread, sel_s[ROWS, i], preferred_element_type=F32)
        by_expert = by_expert[0:8] + by_expert[64:72]
        for q in range(2):
            x_at = xh if q == 0 else 1 - xh
            ids = metas[ROWS, at, x_at][0:8]
            mine = jnp.where(x_at == 0, by_expert[:, :tok], by_expert[:, tok:])
            total = jnp.zeros((8, tok), F32)
            for row in range(8):
                total = total + jnp.where(ids == numbers[row : row + 1], mine[row : row + 1], 0.0)
            cg_s[i, q] = total
            if (i, q) != (0, 0):
                cg_copy(i, q).start()

    for q in (1, 0):
        for p in paths:
            for d in range(2):
                rs_copy(p, q, d, 0).wait_recv()
                step = 1 - 2 * d
                x_at = xh if q == 0 else 1 - xh
                mid = partial_at(p, wrap(line[p] + step), x_at, d)
                mid[...] = (mid[...].astype(F32) + far[p, q, d].astype(F32)).astype(BF16)
                rs_copy(p, q, d, 2).start()
    for q in (1, 0):
        for p in paths:
            for d in range(2):
                for k in (1, 2):
                    rs_copy(p, q, d, k).wait_recv()
            x_at = xh if q == 0 else 1 - xh
            mine = partial_at(p, line[p], x_at)
            for part in range(2):
                rows = pl.ds(part * half, half)
                mine[rows, :] = (
                    mine[rows, :].astype(F32) + near[p, q, 0, part].astype(F32) + near[p, q, 1, part].astype(F32)
                ).astype(BF16)
            fin_copy(p, q).start()

    total = cg_s[0, 0]
    for i, q in others:
        cg_copy(i, q).wait_recv()
        total = total + cg_r[i, q]
    cg_ref[...] = total
    for p in paths:
        for q in range(2):
            fin_copy(p, q).wait_recv()
        out_ref[:, pl.ds(p * cols, cols)] = (final[0, p].astype(F32) + final[1, p].astype(F32)).astype(BF16)

    for p in paths:
        for e in range(2):
            for j in far_first:
                ret_copy(p, e, j).wait_send()
        for q in range(2):
            for d in range(2):
                for k in range(3):
                    rs_copy(p, q, d, k).wait_send()
            fin_copy(p, q).wait_send()
    for j in far_first:
        score_copy(j).wait_send()
    for i, q in others:
        cg_copy(i, q).wait_send()


def on_device(layer_input, out_grad, expert_ids, combine, w_gate, w_up, w_down):
    tok, width = layer_input.shape[1:]
    hidden_units = w_gate.shape[3]
    experts = w_gate.shape[1] * lax.axis_size("ep")
    cap = 3 * tok * expert_ids.shape[2] // (2 * experts)
    slot = 2 * cap
    per_expert = LINE * LINE * slot
    cols = width // 2
    meta = jnp.concatenate([expert_ids[0].astype(F32).T, combine[0].T], axis=0)
    vmem, hbm = pl.BlockSpec(memory_space=pltpu.VMEM), pl.BlockSpec(memory_space=pl.ANY)
    dma = pltpu.SemaphoreType.DMA
    grad, scores = pl.pallas_call(
        functools.partial(kernel, tok, cap, width, hidden_units),
        out_shape=(jax.ShapeDtypeStruct((tok, width), BF16), jax.ShapeDtypeStruct((8, tok), F32)),
        in_specs=[hbm, hbm, vmem, hbm, hbm, hbm],
        out_specs=(vmem, vmem),
        scratch_shapes=[
            pltpu.VMEM((2 * LINE * 2 * tok, width), BF16),
            pltpu.VMEM((2, LINE, 2, 16, tok), F32),
            pltpu.VMEM((2 * 3 * 2 * LINE * slot, width), BF16),
            pltpu.VMEM((2 * 2 * per_expert, width), BF16),
            pltpu.VMEM((2, 2, LINE, LINE * slot, cols), BF16),
            pltpu.VMEM((2, 2, 2, 2, tok // 2, cols), BF16),
            pltpu.VMEM((2, 2, 2, tok // 2, cols), BF16),
            pltpu.VMEM((2, 2, tok, cols), BF16),
            pltpu.VMEM((2, LINE, 8 * slot, 2 * tok), BF16),
            pltpu.VMEM((2, LINE, 2 * tok, 8 * slot), BF16),
            pltpu.VMEM((width, hidden_units), BF16),
            pltpu.VMEM((width, hidden_units), BF16),
            pltpu.VMEM((hidden_units, width), BF16),
            pltpu.VMEM((per_expert, hidden_units), BF16),
            pltpu.VMEM((per_expert, hidden_units), BF16),
            pltpu.VMEM((per_expert, 128), BF16),
            pltpu.VMEM((per_expert, 128), F32),
            pltpu.VMEM((LINE, LINE * slot, 128), BF16),
            pltpu.VMEM((LINE, 2, 8, tok), F32),
            pltpu.VMEM((LINE, 2, 8, tok), F32),
            dma((2, 2)), dma((2, 2)),
            dma((2, 2, 2, 3)), dma((2, 2, 2, 3)),
            dma((2, LINE, 2)), dma((2, LINE, 2)),
            dma((2,)), dma((3,)),
            dma((2, 2, 3, LINE)), dma((2, 2, 3, LINE)),
            dma((2, 2, 3)), dma((2, 2, 3)), dma((2, 2)),
            dma((3,)), dma((3,)),
            dma((LINE, 2)), dma((LINE, 2)),
            dma((2, 2, 2, 3)), dma((2, 2, 2, 3)),
            dma((2, 2)), dma((2, 2)),
        ],
        compiler_params=pltpu.CompilerParams(
            collective_id=0, has_side_effects=True, vmem_limit_bytes=63 << 20
        ),
        cost_estimate=pl.CostEstimate(
            flops=10 * 2 * per_expert * width * hidden_units, bytes_accessed=24 << 20, transcendentals=0
        ),
        name="routed_backward",
    )(layer_input[0], out_grad[0], meta, w_gate[0], w_up[0], w_down[0])
    return grad[None], scores.T.astype(BF16)[None]


def solution(mesh):
    return jax.shard_map(
        on_device,
        mesh=mesh,
        in_specs=(
            P("pp", "ep", None),
            P("pp", "ep", None),
            P("pp", "ep", None),
            P("pp", "ep", None),
            P("pp", "ep", None, None),
            P("pp", "ep", None, None),
            P("pp", "ep", None, None),
        ),
        out_specs=(P("pp", "ep", None), P("pp", "ep", None)),
        check_vma=False,
    )
```

time: 431 us -> 190 us (0.44)
  waiting for transfers between devices: 228 us -> 0 us
  Pallas kernels: 0 us -> 181 us
  matrix products: 73.2 us -> 0 us
  local copies, waits for them, and re-layouts: 49.3 us -> 1.88 us
  starting transfers between devices: 30.8 us -> 0 us
  blocking collectives: 29.2 us -> 0 us
  other arithmetic: 19 us -> 3.23 us
    all_to_all x3 -> x0, waiting for transfers between devices: 228 us -> none  [the longest x1 82.9 us: on_device(): lax.all_to_all(row_grad, 'ep', split_axis=0, concat_axis=0, tiled=True)]
    pallas_call x0 -> x1, Pallas kernels: none -> 181 us  [on_device(): pl.pallas_call(functools.partial(kernel, tok, cap, width, hidden_units),...]
    dot_general x7 -> x0, matrix products: 73.2 us -> none  [the longest x1 14.1 us: expert_work(): jnp.einsum('secf,edf->secd', up_grad, up_w, preferred_element_type=jnp.fl...]
    gather x4 -> x0, local copies, waits for them, and re-layouts: 33.4 us -> none  [the longest x2 14.2 us: dispatch(): return padded[source]]
    all_to_all x1 -> x0, blocking collectives: 29.2 us -> none  [on_device(): lax.all_to_all(score, 'ep', split_axis=0, concat_axis=0, tiled=True)]
    all_to_all x3 -> x0, starting transfers between devices: 25.7 us -> none  [the longest x1 11.1 us: on_device(): lax.all_to_all(send_rows, 'ep', split_axis=0, concat_axis=0, tiled=True)]
    another operation x3 -> x0, other arithmetic: 18.2 us -> none
    convert_element_type x2 -> x0, local copies, waits for them, and re-layouts: 6.66 us -> none  [the longest x1 6.56 us: expert_work(): return (row_grad.astype(jnp.bfloat16), score)]
  transfers between devices with their start and end apart: 4 -> 0, of which waited for: 3 -> 0; matrix products, arithmetic and copies ran while one was open for 11% -> 0% of each run, Pallas kernels for 0% -> 0%
where the time goes in v1:
time: 190 us; the launch traced here: 187 us
  Pallas kernels  181 us (95%)
  other arithmetic  3.23 us (2%)
    pallas_call x1, Pallas kernels, on_device(): pl.pallas_call(functools.partial(kernel, tok, cap, width, hidden_units),...  181 us

profile of v1, /device:TPU:0, one launch (start us, length us, event | category | flops | bytes accessed | tf_op | source)
XLA Modules:
  0.0 186.6 jit_solution(11742727049285220356)
XLA Ops:
  0.6 0.7 convert_bitcast_fusion
  1.3 1.3 pad_maximum_fusion.meta_in
  2.6 180.9 %routed_backward.1 = (bf16[128,2048]{1,0:T(8,128)(2,1)}, f32[8,128]{1,0:T(8,128)}) custom-call(bf16[128,2048]{1,0:T(8,128)(2,1)} %bitcast.22, bf16[128,2048]{1,0:T(8,128)(2,1)} %bitcast.23, f32[16,128]{1,0:T(8,128)} %pad_maximum_fusion.meta_in, bf16[2,2048,768]{2,1,0:T(8,128)(2,1)} %bitcast.19, bf16[2,2048,768]{2,1,0:T(8,128)(2,1)} %bitcast.20, ...), custom_call_target="tpu_custom_call" | custom-call | flops 24159191040 | bytes 25165824 | tf_op jit(solution)/shard_map/routed_backward/pallas_call | solution.py:529
  183.5 1.3 convert_bitcast_fusion.1
  184.8 1.9 %copy.10 = bf16[1,128,2048]{2,1,0:T(8,128)(2,1)} copy(bf16[1,128,2048]{2,1,0:T(8,128)(2,1)} %bitcast.17) | data formatting | bytes 1048576

commit v2 on v1

v2 whole, which is shorter than its diff:
```python
import functools

import jax
import jax.numpy as jnp
from jax import lax
from jax.experimental import pallas as pl
from jax.experimental.pallas import tpu as pltpu
from jax.sharding import PartitionSpec as P

MESH = pl.DeviceIdType.MESH
LINE = 4
BF16 = jnp.bfloat16
F32 = jnp.float32
ROWS, GRADS = 0, 1


def kernel(
    tok, cap, width, hidden_units,
    rows_in, grads_in, ids_in, share_in, gate_w, up_w, down_w,
    out_ref, cg_ref,
    blocks, metas, staged, arrived, returned, near, far, beside, final,
    sel_s, wsel_s, wg, wu, wd, gg_s, ug_s, score_0, score_s, score_acc, score_r, cg_s, cg_r,
    block_send, x_recv, xn_recv, ag_recv, ag_far, meta_send, meta_recv, own_sem, w_sem,
    fwd_send, fwd_recv, ret_send, ret_recv, ret_own, sc_send, sc_recv, cg_send, cg_recv,
    rs_send, rs_recv, far_recv, beside_recv, fin_send, fin_recv,
):
    slot = 2 * cap
    group = LINE * slot
    half = tok // 2
    cols = width // 2
    pair = 2 * tok
    per_expert = LINE * group
    pp, ep = lax.axis_index("pp"), lax.axis_index("ep")
    z, xh, y = ep // 8, (ep // 4) % 2, ep % 4
    line, cross = (z, y), (y, z)
    inputs = (rows_in, grads_in)

    def wrap(v):
        return lax.rem(v + LINE, LINE)

    def member(p, i):
        c = line[p]
        return (c, (c // 2) * 2 + 1 - c % 2, wrap(c + 2), 3 - c)[i]

    def column(q):
        return xh if q == 0 else 1 - xh

    def chunk(p, s):
        at = line[p] // 2 if s % 2 == 0 else 1 - line[p] // 2
        return column(s // 2), at

    chunks = range(4)

    def device(p, line_at, x_at, cross_at, section=None):
        z_at, y_at = (line_at, cross_at) if p == ROWS else (cross_at, line_at)
        return {"pp": pp if section is None else section, "ep": z_at * 8 + x_at * 4 + y_at}

    def remote(src, dst, send, recv, to):
        return pltpu.make_async_remote_copy(
            src_ref=src, dst_ref=dst, send_sem=send, recv_sem=recv, device_id=to, device_id_type=MESH
        )

    def drain(ref, sem):
        pltpu.make_async_copy(ref, ref, sem).wait()

    def meta_at(p, line_at, x_at):
        return (p * LINE + line_at) * 2 + x_at

    def place(p, line_at, x_at, part=None):
        start = ((p * 2 + x_at) * LINE + line_at) * tok
        if part is None:
            return blocks.at[pl.ds(pl.multiple_of(start, tok), tok), :]
        return blocks.at[pl.ds(pl.multiple_of(start + part * half, half), half), :]

    before, after = lax.rem(pp + 3, 4), lax.rem(pp + 1, 4)
    peers = [device(ROWS, member(ROWS, i), column(q), y) for i in range(LINE) for q in range(2)][1:]
    peers += [device(GRADS, member(GRADS, i), column(q), z) for i in range(1, LINE) for q in range(2)]
    peers += [device(ROWS, z, x_at, y, s) for x_at in (xh, 1 - xh) for s in (before, after)]
    barrier = pltpu.get_barrier_semaphore()
    for peer in peers:
        pl.semaphore_signal(barrier, inc=1, device_id=peer, device_id_type=MESH)
    pl.semaphore_wait(barrier, len(peers))

    def own_half(p, part):
        return inputs[p].at[pl.ds(pl.multiple_of(part * half, half), half), :]

    def x_copy(p, part):
        return remote(
            own_half(p, part), place(p, line[p], xh, part), block_send, x_recv.at[p],
            device(p, line[p], 1 - xh, cross[p]),
        )

    def x_wait(p):
        drain(place(p, line[p], 1 - xh), x_recv.at[p])

    def xn_copy(p, d, k):
        dst = place(p, wrap(line[p] - (1 - 2 * d)), xh, ag_part(d, k))
        return remote(dst, dst, block_send, xn_recv.at[p, d, k], device(p, line[p], 1 - xh, cross[p]))

    def xn_wait(p, d, k):
        drain(place(p, wrap(line[p] - (1 - 2 * d)), 1 - xh, ag_part(d, k)), xn_recv.at[p, d, k])

    def ag_part(d, k):
        return lax.rem(d + k, 2) if k < 2 else d

    def ag_copy(p, q, d, k):
        step = 1 - 2 * d
        part = ag_part(d, k)
        x_at = xh if q == 0 else 1 - xh
        at = line[p] if k < 2 else wrap(line[p] - step)
        dst = place(p, at, x_at, part)
        src = own_half(p, part) if q == 0 and k < 2 else dst
        sem = ag_recv.at[p, d, k] if k < 2 else ag_far.at[p, q]
        return remote(src, dst, block_send, sem, device(p, wrap(line[p] + step), xh, cross[p]))

    def ag_wait(p, d, k):
        drain(place(p, wrap(line[p] - (1 - 2 * d)), xh, ag_part(d, k)), ag_recv.at[p, d, k])

    def ag_wait_far(p, q):
        drain(place(p, wrap(line[p] + 2), column(q)), ag_far.at[p, q])

    def meta_copy(p, i, q):
        mine = metas.at[meta_at(p, line[p], xh)]
        return remote(mine, mine, meta_send, meta_recv, device(p, member(p, i), column(q), cross[p]))

    others = [(i, q) for i in range(LINE) for q in range(2) if (i, q) != (0, 0)]
    paths = (ROWS, GRADS)
    for p in paths:
        metas[meta_at(p, line[p], xh), 0:8] = ids_in[...].astype(F32)
        metas[meta_at(p, line[p], xh), 8:16] = share_in[...]
        for i, q in others:
            meta_copy(p, i, q).start()
    for p in paths:
        for part in range(2):
            x_copy(p, part).start()
    for k in range(2):
        for p in paths:
            for d in range(2):
                ag_copy(p, 0, d, k).start()
    own = []
    for p in paths:
        own.append(pltpu.make_async_copy(inputs[p], place(p, line[p], xh), own_sem.at[p]))
        own[-1].start()

    def weights(e):
        return [
            pltpu.make_async_copy(src.at[e], dst, w_sem.at[i])
            for i, (src, dst) in enumerate(((gate_w, wg), (up_w, wu), (down_w, wd)))
        ]

    for copy in weights(0):
        copy.start()
    all_metas = metas.at[pl.ds(0, 2 * len(others))]
    drain(all_metas, meta_recv)

    def expert_numbers(p):
        row = lax.broadcasted_iota(jnp.int32, (8, tok), 0)
        e, across = row // LINE, (row + cross[p]) % LINE
        if p == ROWS:
            return 16 * z + 8 * xh + 2 * across + e
        return 16 * across + 8 * xh + 2 * y + e

    earlier = (
        lax.broadcasted_iota(jnp.int32, (tok, tok), 0) < lax.broadcasted_iota(jnp.int32, (tok, tok), 1)
    ).astype(F32).astype(BF16)
    rank_no = lax.broadcasted_iota(jnp.int32, (cap, tok), 0).astype(F32)
    nothing = jnp.zeros((cap, tok), F32)

    for p in paths:
        numbers = expert_numbers(p).astype(F32)

        def build(i, carry, p=p, numbers=numbers):
            x_at = lax.rem(xh + i // 2, 2)
            own_pair = line[p] // 2
            first_line = 2 * lax.rem(own_pair + i % 2, 2)
            weight, rank = [], []
            for h in range(2):
                meta = metas[meta_at(p, first_line + h, x_at)]
                named = jnp.zeros((8, tok), F32)
                share = jnp.zeros((8, tok), F32)
                for k in range(8):
                    same = meta[k : k + 1, :] == numbers
                    named = named + jnp.where(same, 1.0, 0.0)
                    share = share + jnp.where(same, meta[8 + k : 9 + k, :], 0.0)
                before_it = jnp.dot(named.astype(BF16), earlier, preferred_element_type=F32)
                rank.append(jnp.where(named > 0.0, before_it, -1.0))
                weight.append(share)
            hot, hot_w = [], []
            for row in range(8):
                for h in range(2):
                    hit = rank[h][row : row + 1, :] == rank_no
                    one = jnp.where(hit, 1.0, 0.0)
                    scaled = jnp.where(hit, weight[h][row : row + 1, :], 0.0)
                    hot.append(jnp.concatenate([one, nothing] if h == 0 else [nothing, one], axis=1))
                    hot_w.append(jnp.concatenate([scaled, nothing] if h == 0 else [nothing, scaled], axis=1))
            sel_s[p, i] = jnp.concatenate(hot, axis=0).astype(BF16)
            wsel_s[p, i] = jnp.concatenate(hot_w, axis=0).T.astype(BF16)
            return carry

        lax.fori_loop(0, LINE, build, 0)

    def arrived_at(p, e, from_cross, x_at, pair_at):
        start = (p * 2 + e) * per_expert + ((x_at * LINE + from_cross) * 2 + pair_at) * slot
        return arrived.at[pl.ds(pl.multiple_of(start, 16), slot), :]

    def fwd_copy(p, e, j, s):
        return remote(
            staged.at[pl.ds((((p * 3 + j - 1) * 2 + e) * 4 + s) * slot, slot), :],
            arrived_at(p, e, cross[p], *chunk(p, s)), fwd_send, fwd_recv.at[p, e],
            device(p, line[p], xh, wrap(cross[p] + j)),
        )

    tile = 512

    def select(p, s):
        x_at, pair_at = chunk(p, s)
        start = pl.multiple_of(((p * 2 + x_at) * 2 + pair_at) * pair, pair)

        @pl.loop(0, width // tile)
        def _(n):
            lanes = pl.ds(pl.multiple_of(n * tile, tile), tile)
            picked = jnp.dot(
                sel_s[p, s], blocks[pl.ds(start, pair), lanes], preferred_element_type=F32
            ).astype(BF16)
            for e in range(2):
                for j in range(LINE):
                    part = picked[(e * LINE + j) * slot : (e * LINE + j + 1) * slot]
                    if j == 0:
                        arrived_at(p, e, cross[p], x_at, pair_at)[:, lanes] = part
                    else:
                        first = (((p * 3 + j - 1) * 2 + e) * 4 + s) * slot
                        staged[pl.ds(first, slot), lanes] = part

    far_first = (2, 1, 3)

    def send_selected(p, e, s):
        for j in far_first:
            fwd_copy(p, e, j, s).start()

    near_way = [1 - line[p] % 2 for p in paths]
    far_way = [line[p] % 2 for p in paths]
    for p in paths:
        for d in (near_way[p], far_way[p]):
            ag_wait(p, d, 0)
            ag_copy(p, 0, d, 2).start()
            xn_copy(p, d, 0).start()
    for p in paths:
        ag_wait(p, near_way[p], 1)
        xn_copy(p, near_way[p], 1).start()
        own[p].wait()
        select(p, 0)
        for e in range(2):
            send_selected(p, e, 0)
    for p in paths:
        ag_wait(p, far_way[p], 1)
        xn_copy(p, far_way[p], 1).start()
        ag_wait_far(p, 0)
        select(p, 1)
        for e in range(2):
            send_selected(p, e, 1)
    for p in paths:
        x_wait(p)
        xn_wait(p, near_way[p], 0)
        ag_copy(p, 1, near_way[p], 2).start()
        xn_wait(p, near_way[p], 1)
        select(p, 2)
        send_selected(p, 0, 2)
    for p in paths:
        xn_wait(p, far_way[p], 0)
        ag_copy(p, 1, far_way[p], 2).start()
    for p in paths:
        xn_wait(p, far_way[p], 1)
        ag_wait_far(p, 1)
        select(p, 3)
        send_selected(p, 0, 3)
    for s in (2, 3):
        for p in paths:
            send_selected(p, 1, s)
    drain(blocks.at[pl.ds(0, 14 * tok), :], block_send)
    drain(all_metas, meta_send)

    def grad_rows(p, e, j, q):
        start = e * per_expert + wrap(cross[p] + j) * group + column(q) * (group // 2)
        return blocks.at[pl.ds(pl.multiple_of(start, 16), group // 2), pl.ds(p * cols, cols)]

    def ret_copy(p, e, j, q):
        return remote(
            grad_rows(p, e, j, q), returned.at[p, q, LINE - j, e], ret_send, ret_recv.at[p, q],
            device(p, line[p], xh, wrap(cross[p] + j)),
        )

    def own_return(p, e, q):
        return pltpu.make_async_copy(grad_rows(p, e, 0, q), returned.at[p, q, 0, e], ret_own.at[p, q])

    transposed = (((1,), (1,)), ((), ()))
    f_tile = 256
    d_tile = 256
    low = lax.broadcasted_iota(jnp.int32, (per_expert, 128), 1) < 64

    def reorder(value):
        return jnp.concatenate(
            [
                value[((x_at * LINE + b) * LINE + a) * cap : ((x_at * LINE + b) * LINE + a + 1) * cap]
                for x_at in range(2) for a in range(LINE) for b in range(LINE)
            ],
            axis=0,
        )

    def to_return(value, p):
        parts = []
        for dst in range(LINE):
            for x_at in range(2):
                for src in range(LINE):
                    y_at, z_at = (dst, src) if p == ROWS else (src, dst)
                    first = ((x_at * LINE + y_at) * LINE + z_at) * cap
                    parts.append(value[first : first + cap])
        return jnp.concatenate(parts, axis=0)

    def expert(e):
        for copy in weights(e):
            copy.wait()
        for p in paths:
            drain(arrived.at[pl.ds((p * 2 + e) * per_expert, 3 * group), :], fwd_recv.at[p, e])
        row_at = pl.ds(e * per_expert, per_expert)
        grad_at = pl.ds((2 + e) * per_expert, per_expert)

        @pl.loop(0, hidden_units // f_tile)
        def _(n):
            units = pl.ds(pl.multiple_of(n * f_tile, f_tile), f_tile)
            gate = jnp.dot(arrived[row_at, :], wg[:, units], preferred_element_type=F32)
            up = jnp.dot(arrived[row_at, :], wu[:, units], preferred_element_type=F32)
            back = lax.dot_general(arrived[grad_at, :], wd[units, :], transposed, preferred_element_type=F32)
            back = reorder(back)
            sigma = jax.nn.sigmoid(gate)
            active = gate * sigma
            hidden = (active * up).astype(BF16).astype(F32)
            term = hidden * back
            gg_s[:, units] = (back * up * sigma * (1.0 + gate * (1.0 - sigma))).astype(BF16)
            ug_s[:, units] = (back * active).astype(BF16)
            term = term[:, :128] + term[:, 128:]

            @pl.when(n == 0)
            def _():
                score_acc[...] = term

            @pl.when(n > 0)
            def _():
                score_acc[...] += term

        for p in paths:

            @pl.loop(0, cols // d_tile)
            def _(n, p=p):
                lanes = pl.ds(pl.multiple_of(p * cols + n * d_tile, d_tile), d_tile)
                grad = lax.dot_general(gg_s[...], wg[lanes, :], transposed, preferred_element_type=F32)
                grad = grad + lax.dot_general(ug_s[...], wu[lanes, :], transposed, preferred_element_type=F32)
                blocks[pl.ds(e * per_expert, per_expert), lanes] = to_return(grad, p).astype(BF16)

            for q in (1, 0):
                for j in far_first:
                    ret_copy(p, e, j, q).start()
                own_return(p, e, q).start()

        score = jnp.broadcast_to(jnp.sum(score_acc[...], axis=1, keepdims=True), (per_expert, 128))
        if e == 0:
            score_0[...] = score
        else:
            score_0[...] = jnp.where(low, score_0[...], score)

    def score_copy(j):
        return remote(
            score_s.at[wrap(y + j)], score_r.at[LINE - j], sc_send, sc_recv,
            device(ROWS, z, xh, wrap(y + j)),
        )

    expert(0)
    for copy in weights(1):
        copy.start()
    expert(1)
    blank = jnp.zeros((128 - slot, 128), F32)
    first = lax.broadcasted_iota(jnp.int32, (8, 128), 0) < 4
    for y_src in range(LINE):
        for t in range(4):
            start = ((t // 2 * LINE + y_src) * 2 + t % 2) * slot
            turned = jnp.concatenate([score_0[start : start + slot, :], blank], axis=0).T
            score_s[y_src, :, t * 128 : (t + 1) * 128] = jnp.where(first, turned[0:8], turned[64:72])
    for j in far_first:
        score_copy(j).start()
    score_r[0] = score_s[y]
    drain(staged, fwd_send)

    def partial_at(p, at, x_at, part=None):
        start = (x_at * LINE + at) * tok
        lanes = pl.ds(p * cols, cols)
        if part is None:
            return staged.at[pl.ds(pl.multiple_of(start, tok), tok), lanes]
        return staged.at[pl.ds(pl.multiple_of(start + part * half, half), half), lanes]

    def combine(p, s):
        x_at, pair_at = chunk(p, s)
        take = pl.ds(pl.multiple_of(pair_at * slot, 16), slot)
        gathered = jnp.concatenate([returned[p, s // 2, j, e, take, :] for e in range(2) for j in range(LINE)], axis=0)
        rows = pl.ds(pl.multiple_of((x_at * 2 + pair_at) * pair, pair), pair)
        for n in range(cols // tile):
            staged[rows, pl.ds(p * cols + n * tile, tile)] = jnp.dot(
                wsel_s[p, s], gathered[:, n * tile : (n + 1) * tile], preferred_element_type=F32
            ).astype(BF16)

    def rs_copy(p, d, k):
        step = 1 - 2 * d
        at = wrap(line[p] + 2) if k == 0 else wrap(line[p] + step)
        part = 1 - d if k == 1 else d
        dst = far.at[p, d] if k == 0 else near.at[p, 0, d, pl.ds(pl.multiple_of(part * half, half), half)]
        return remote(
            partial_at(p, at, xh, part), dst, rs_send, far_recv.at[p] if k == 0 else rs_recv.at[p, 0],
            device(p, wrap(line[p] + step), xh, cross[p]),
        )

    def rs_whole(p, d):
        step = 1 - 2 * d
        return remote(
            partial_at(p, wrap(line[p] + step), 1 - xh), near.at[p, 1, d], rs_send, rs_recv.at[p, 1],
            device(p, wrap(line[p] + step), xh, cross[p]),
        )

    def beside_copy(p):
        return remote(
            partial_at(p, wrap(line[p] + 2), 1 - xh), beside.at[p], rs_send, beside_recv.at[p],
            device(p, line[p], 1 - xh, cross[p]),
        )

    def fin_copy(p, q):
        x_at = xh if q == 0 else 1 - xh
        return remote(
            partial_at(p, line[p], x_at), final.at[q, p], fin_send, fin_recv,
            device(p, line[p], x_at, cross[p], before),
        )

    def cg_copy(i, q):
        return remote(
            cg_s.at[2 * i + q], cg_r.at[2 * i + q - 1], cg_send, cg_recv,
            device(ROWS, member(ROWS, i), column(q), y),
        )

    def sum_up(p, q):
        mine = partial_at(p, line[p], column(q))
        mine[...] = (
            mine[...].astype(F32) + near[p, q, 0].astype(F32) + near[p, q, 1].astype(F32)
        ).astype(BF16)

    def wait_returned(p, q):
        drain(returned.at[p, q, pl.ds(1, 3)], ret_recv.at[p, q])
        drain(returned.at[p, q, 0], ret_own.at[p, q])

    for p in paths:
        wait_returned(p, 1)
        combine(p, 3)
        beside_copy(p).start()
        rs_whole(p, near_way[p]).start()
        combine(p, 2)
        rs_whole(p, far_way[p]).start()
    for p in paths:
        wait_returned(p, 0)
        combine(p, 1)
        rs_copy(p, near_way[p], 1).start()
        drain(beside.at[p], beside_recv.at[p])
        mine = partial_at(p, wrap(line[p] + 2), xh)
        mine[...] = (mine[...].astype(F32) + beside[p].astype(F32)).astype(BF16)
        for d in range(2):
            rs_copy(p, d, 0).start()
        combine(p, 0)
        rs_copy(p, far_way[p], 1).start()
    for p in paths:
        drain(near.at[p, 1], rs_recv.at[p, 1])
        sum_up(p, 1)
        fin_copy(p, 1).start()

    drain(score_r.at[pl.ds(1, 3)], sc_recv)
    row = lax.broadcasted_iota(jnp.int32, (8, 128), 0)
    numbers = expert_numbers(ROWS).astype(F32)
    pad = jnp.zeros((128 - slot, pair), BF16)
    for s in chunks:
        x_at, pair_at = chunk(ROWS, s)
        take = pl.ds(pl.multiple_of((x_at * 2 + pair_at) * 128, 128), 128)
        by_expert = jnp.zeros((8, pair), F32)
        for j in range(LINE):
            tile_j = score_r[j, :, take]
            for e in range(2):
                block = e * LINE + j
                mine = jnp.where(row == block, tile_j, 0.0).astype(BF16)
                hot = jnp.concatenate([sel_s[ROWS, s, block * slot : (block + 1) * slot, :], pad], axis=0)
                by_expert = by_expert + jnp.dot(mine, hot, preferred_element_type=F32)
        for m in range(2):
            i, q = 2 * (s % 2) + m, s // 2
            ids = metas[meta_at(ROWS, member(ROWS, i), x_at), 0:8]
            mine = jnp.where(lax.rem(z + m, 2) == 0, by_expert[:, :tok], by_expert[:, tok:])
            total = jnp.zeros((8, tok), F32)
            for block in range(8):
                total = total + jnp.where(ids == numbers[block : block + 1], mine[block : block + 1], 0.0)
            cg_s[2 * i + q] = total
            if (i, q) != (0, 0):
                cg_copy(i, q).start()

    for p in paths:
        drain(far.at[p], far_recv.at[p])
        for d in range(2):
            mid = partial_at(p, wrap(line[p] + 1 - 2 * d), xh, d)
            mid[...] = (mid[...].astype(F32) + far[p, d].astype(F32)).astype(BF16)
            rs_copy(p, d, 2).start()
    for p in paths:
        drain(near.at[p, 0], rs_recv.at[p, 0])
        sum_up(p, 0)
        fin_copy(p, 0).start()

    drain(cg_r, cg_recv)
    total = cg_s[0]
    for i in range(len(others)):
        total = total + cg_r[i]
    cg_ref[...] = total.astype(BF16)
    drain(final, fin_recv)
    for p in paths:
        out_ref[:, pl.ds(p * cols, cols)] = (final[0, p].astype(F32) + final[1, p].astype(F32)).astype(BF16)

    drain(blocks.at[pl.ds(0, 6 * group), :], ret_send)
    drain(staged.at[pl.ds(0, 12 * tok), pl.ds(0, cols)], rs_send)
    drain(final, fin_send)
    drain(score_r.at[pl.ds(1, 3)], sc_send)
    drain(cg_r, cg_send)


def on_device(layer_input, out_grad, expert_ids, combine, w_gate, w_up, w_down):
    tok, width = layer_input.shape[1:]
    hidden_units = w_gate.shape[3]
    experts = w_gate.shape[1] * lax.axis_size("ep")
    cap = 3 * tok * expert_ids.shape[2] // (2 * experts)
    slot = 2 * cap
    per_expert = LINE * LINE * slot
    cols = width // 2
    vmem, hbm = pl.BlockSpec(memory_space=pltpu.VMEM), pl.BlockSpec(memory_space=pl.ANY)
    dma = pltpu.SemaphoreType.DMA
    grad, scores = pl.pallas_call(
        functools.partial(kernel, tok, cap, width, hidden_units),
        out_shape=(jax.ShapeDtypeStruct((tok, width), BF16), jax.ShapeDtypeStruct((8, tok), BF16)),
        in_specs=[hbm, hbm, vmem, vmem, hbm, hbm, hbm],
        out_specs=(vmem, vmem),
        scratch_shapes=[
            pltpu.VMEM((2 * LINE * 2 * tok, width), BF16),
            pltpu.VMEM((2 * LINE * 2, 16, tok), F32),
            pltpu.VMEM((2 * 3 * 2 * LINE * slot, width), BF16),
            pltpu.VMEM((2 * 2 * per_expert, width), BF16),
            pltpu.VMEM((2, 2, LINE, 2, 2 * slot, cols), BF16),
            pltpu.VMEM((2, 2, 2, tok, cols), BF16),
            pltpu.VMEM((2, 2, tok // 2, cols), BF16),
            pltpu.VMEM((2, tok, cols), BF16),
            pltpu.VMEM((2, 2, tok, cols), BF16),
            pltpu.VMEM((2, LINE, 8 * slot, 2 * tok), BF16),
            pltpu.VMEM((2, LINE, 2 * tok, 8 * slot), BF16),
            pltpu.VMEM((width, hidden_units), BF16),
            pltpu.VMEM((width, hidden_units), BF16),
            pltpu.VMEM((hidden_units, width), BF16),
            pltpu.VMEM((per_expert, hidden_units), BF16),
            pltpu.VMEM((per_expert, hidden_units), BF16),
            pltpu.VMEM((per_expert, 128), F32),
            pltpu.VMEM((LINE, 8, LINE * 128), F32),
            pltpu.VMEM((per_expert, 128), F32),
            pltpu.VMEM((LINE, 8, LINE * 128), F32),
            pltpu.VMEM((LINE * 2, 8, tok), F32),
            pltpu.VMEM((LINE * 2 - 1, 8, tok), F32),
            dma, dma((2,)), dma((2, 2, 2)), dma((2, 2, 2)), dma((2, 2)), dma, dma, dma((2,)), dma((3,)),
            dma, dma((2, 2)), dma, dma((2, 2)), dma((2, 2)), dma, dma, dma, dma,
            dma, dma((2, 2)), dma((2,)), dma((2,)), dma, dma,
        ],
        compiler_params=pltpu.CompilerParams(
            collective_id=0, has_side_effects=True, vmem_limit_bytes=63 << 20
        ),
        cost_estimate=pl.CostEstimate(
            flops=10 * 2 * per_expert * width * hidden_units, bytes_accessed=24 << 20, transcendentals=0
        ),
        name="routed_backward",
    )(layer_input[0], out_grad[0], expert_ids[0].T, combine[0].T, w_gate[0], w_up[0], w_down[0])
    return grad[None], scores.T[None]


def solution(mesh):
    return jax.shard_map(
        on_device,
        mesh=mesh,
        in_specs=(
            P("pp", "ep", None),
            P("pp", "ep", None),
            P("pp", "ep", None),
            P("pp", "ep", None),
            P("pp", "ep", None, None),
            P("pp", "ep", None, None),
            P("pp", "ep", None, None),
        ),
        out_specs=(P("pp", "ep", None), P("pp", "ep", None)),
        check_vma=False,
    )
```

time: 190 us -> 177 us (0.932)
  Pallas kernels: 181 us -> 171 us
  other arithmetic: 3.23 us -> 0 us
    pallas_call x1, Pallas kernels: 181 us -> 171 us  [on_device(): pl.pallas_call(functools.partial(kernel, tok, cap, width, hidden_units),...]
where the time goes in v2:
time: 177 us; the launch traced here: 175 us
  Pallas kernels  171 us (97%)
  local copies, waits for them, and re-layouts  3.13 us (2%)
    pallas_call x1, Pallas kernels, on_device(): pl.pallas_call(functools.partial(kernel, tok, cap, width, hidden_units),...  171 us

profile of v2, /device:TPU:0, one launch (start us, length us, event | category | flops | bytes accessed | tf_op | source)
XLA Modules:
  0.0 174.8 jit_solution(12518314130001224661)
XLA Ops:
  0.6 171.0 %routed_backward.1 = (bf16[128,2048]{1,0:T(8,128)(2,1)}, bf16[8,128]{1,0:T(8,128)(2,1)}) custom-call(bf16[128,2048]{1,0:T(8,128)(2,1)} %bitcast.20, bf16[128,2048]{1,0:T(8,128)(2,1)} %bitcast.21, s32[8,128]{1,0:T(8,128)} %bitcast.22, f32[8,128]{1,0:T(8,128)} %bitcast.23, bf16[2,2048,768]{2,1,0:T(8,128)(2,1)} %bitcast.17, bf16[2,2048,768]{2,1,0:T(8,128)(2,1)} %bitcast.18, ...), custom_call_target="tpu_custom_call" | custom-call | flops 24159191040 | bytes 25165824 | tf_op jit(solution)/shard_map/routed_backward/pallas_call | solution.py:541
  171.7 1.9 %copy.11 = bf16[1,128,2048]{2,1,0:T(8,128)(2,1)} copy(bf16[1,128,2048]{2,1,0:T(8,128)(2,1)} %bitcast.15) | data formatting | bytes 1048576
  173.6 1.3 copy.12

commit v3 on v2

--- a/solution.py
+++ b/solution.py
@@ -18,7 +18,7 @@
     tok, cap, width, hidden_units,
     rows_in, grads_in, ids_in, share_in, gate_w, up_w, down_w,
     out_ref, cg_ref,
-    blocks, metas, staged, arrived, returned, near, far, beside, final,
+    blocks, early, metas, staged, arrived, returned, near, far, beside, final,
     sel_s, wsel_s, wg, wu, wd, gg_s, ug_s, score_0, score_s, score_acc, score_r, cg_s, cg_r,
     block_send, x_recv, xn_recv, ag_recv, ag_far, meta_send, meta_recv, own_sem, w_sem,
     fwd_send, fwd_recv, ret_send, ret_recv, ret_own, sc_send, sc_recv, cg_send, cg_recv,
@@ -30,6 +30,7 @@
     cols = width // 2
     pair = 2 * tok
     per_expert = LINE * group
+    part_rows = per_expert // 2
     pp, ep = lax.axis_index("pp"), lax.axis_index("ep")
     z, xh, y = ep // 8, (ep // 4) % 2, ep % 4
     line, cross = (z, y), (y, z)
@@ -206,7 +207,7 @@
     def fwd_copy(p, e, j, s):
         return remote(
             staged.at[pl.ds((((p * 3 + j - 1) * 2 + e) * 4 + s) * slot, slot), :],
-            arrived_at(p, e, cross[p], *chunk(p, s)), fwd_send, fwd_recv.at[p, e],
+            arrived_at(p, e, cross[p], *chunk(p, s)), fwd_send, fwd_recv.at[p, e, s // 2],
             device(p, line[p], xh, wrap(cross[p] + j)),
         )
 
@@ -237,29 +238,114 @@
         for j in far_first:
             fwd_copy(p, e, j, s).start()
 
+    def grad_rows(p, e, q, size, start):
+        if (e, q) == (0, 0):
+            return early.at[pl.ds(start, size), pl.ds(p * cols, cols)]
+        base = {(0, 1): 0, (1, 1): 1, (1, 0): 2}[e, q] * part_rows
+        return blocks.at[pl.ds(pl.multiple_of(base + start, 16), size), pl.ds(p * cols, cols)]
+
+    def grads_for(p, e, q, j):
+        return grad_rows(p, e, q, group // 2, pl.multiple_of(wrap(cross[p] + j) * (group // 2), 16))
+
+    def ret_copy(p, e, j, q):
+        return remote(
+            grads_for(p, e, q, j), returned.at[p, q, LINE - j, e], ret_send, ret_recv.at[p, q],
+            device(p, line[p], xh, wrap(cross[p] + j)),
+        )
+
+    def own_return(p, e, q):
+        return pltpu.make_async_copy(grads_for(p, e, q, 0), returned.at[p, q, 0, e], ret_own.at[p, q])
+
+    transposed = (((1,), (1,)), ((), ()))
+    f_tile = 256
+    d_tile = 256
+    low = lax.broadcasted_iota(jnp.int32, (part_rows, 128), 1) < 64
+
+    def turn(value):
+        blocks_of = [value[(a * LINE + b) * cap : (a * LINE + b + 1) * cap] for b in range(LINE) for a in range(LINE)]
+        return jnp.concatenate(blocks_of, axis=0)
+
+    def expert(e, q):
+        for p in paths:
+            drain(arrived.at[pl.ds((p * 2 + e) * per_expert, 3 * group // 2), :], fwd_recv.at[p, e, q])
+        offset = column(q) * part_rows
+        row_at = pl.ds(pl.multiple_of(e * per_expert + offset, part_rows), part_rows)
+        grad_at = pl.ds(pl.multiple_of((2 + e) * per_expert + offset, part_rows), part_rows)
+
+        @pl.loop(0, hidden_units // f_tile)
+        def _(n):
+            units = pl.ds(pl.multiple_of(n * f_tile, f_tile), f_tile)
+            gate = jnp.dot(arrived[row_at, :], wg[:, units], preferred_element_type=F32)
+            up = jnp.dot(arrived[row_at, :], wu[:, units], preferred_element_type=F32)
+            back = lax.dot_general(arrived[grad_at, :], wd[units, :], transposed, preferred_element_type=F32)
+            back = turn(back)
+            sigma = jax.nn.sigmoid(gate)
+            active = gate * sigma
+            hidden = (active * up).astype(BF16).astype(F32)
+            term = hidden * back
+            gg_s[:, units] = (back * up * sigma * (1.0 + gate * (1.0 - sigma))).astype(BF16)
+            ug_s[:, units] = (back * active).astype(BF16)
+            term = term[:, :128] + term[:, 128:]
+
+            @pl.when(n == 0)
+            def _():
+                score_acc[...] = term
+
+            @pl.when(n > 0)
+            def _():
+                score_acc[...] += term
+
+        for p in paths:
+
+            @pl.loop(0, cols // d_tile)
+            def _(n, p=p):
+                lanes = pl.ds(pl.multiple_of(p * cols + n * d_tile, d_tile), d_tile)
+                grad = lax.dot_general(gg_s[...], wg[lanes, :], transposed, preferred_element_type=F32)
+                grad = grad + lax.dot_general(ug_s[...], wu[lanes, :], transposed, preferred_element_type=F32)
+                grad = (grad if p == ROWS else turn(grad)).astype(BF16)
+                grad_rows(p, e, q, part_rows, 0)[:, pl.ds(pl.multiple_of(n * d_tile, d_tile), d_tile)] = grad
+
+            for j in far_first:
+                ret_copy(p, e, j, q).start()
+            own_return(p, e, q).start()
+
+        score = jnp.broadcast_to(jnp.sum(score_acc[...], axis=1, keepdims=True), (part_rows, 128))
+        rows = pl.ds(pl.multiple_of(offset, part_rows), part_rows)
+        if e == 0:
+            score_0[rows, :] = score
+        else:
+            score_0[rows, :] = jnp.where(low, score_0[rows, :], score)
+
     near_way = [1 - line[p] % 2 for p in paths]
     far_way = [line[p] % 2 for p in paths]
     for p in paths:
-        for d in (near_way[p], far_way[p]):
-            ag_wait(p, d, 0)
-            ag_copy(p, 0, d, 2).start()
-            xn_copy(p, d, 0).start()
+        ag_wait(p, near_way[p], 0)
+        ag_copy(p, 0, near_way[p], 2).start()
+        xn_copy(p, near_way[p], 0).start()
+        ag_wait(p, far_way[p], 0)
+        ag_copy(p, 0, far_way[p], 2).start()
     for p in paths:
         ag_wait(p, near_way[p], 1)
         xn_copy(p, near_way[p], 1).start()
         own[p].wait()
         select(p, 0)
-        for e in range(2):
-            send_selected(p, e, 0)
+        send_selected(p, 0, 0)
     for p in paths:
         ag_wait(p, far_way[p], 1)
-        xn_copy(p, far_way[p], 1).start()
         ag_wait_far(p, 0)
         select(p, 1)
-        for e in range(2):
-            send_selected(p, e, 1)
+        send_selected(p, 0, 1)
+    for s in (0, 1):
+        for p in paths:
+            send_selected(p, 1, s)
     for p in paths:
         x_wait(p)
+        for k in range(2):
+            xn_copy(p, far_way[p], k).start()
+    for copy in weights(0):
+        copy.wait()
+    expert(0, 0)
+    for p in paths:
         xn_wait(p, near_way[p], 0)
         ag_copy(p, 1, near_way[p], 2).start()
         xn_wait(p, near_way[p], 1)
@@ -279,104 +365,19 @@
     drain(blocks.at[pl.ds(0, 14 * tok), :], block_send)
     drain(all_metas, meta_send)
 
-    def grad_rows(p, e, j, q):
-        start = e * per_expert + wrap(cross[p] + j) * group + column(q) * (group // 2)
-        return blocks.at[pl.ds(pl.multiple_of(start, 16), group // 2), pl.ds(p * cols, cols)]
-
-    def ret_copy(p, e, j, q):
-        return remote(
-            grad_rows(p, e, j, q), returned.at[p, q, LINE - j, e], ret_send, ret_recv.at[p, q],
-            device(p, line[p], xh, wrap(cross[p] + j)),
-        )
-
-    def own_return(p, e, q):
-        return pltpu.make_async_copy(grad_rows(p, e, 0, q), returned.at[p, q, 0, e], ret_own.at[p, q])
-
-    transposed = (((1,), (1,)), ((), ()))
-    f_tile = 256
-    d_tile = 256
-    low = lax.broadcasted_iota(jnp.int32, (per_expert, 128), 1) < 64
-
-    def reorder(value):
-        return jnp.concatenate(
-            [
-                value[((x_at * LINE + b) * LINE + a) * cap : ((x_at * LINE + b) * LINE + a + 1) * cap]
-                for x_at in range(2) for a in range(LINE) for b in range(LINE)
-            ],
-            axis=0,
-        )
-
-    def to_return(value, p):
-        parts = []
-        for dst in range(LINE):
-            for x_at in range(2):
-                for src in range(LINE):
-                    y_at, z_at = (dst, src) if p == ROWS else (src, dst)
-                    first = ((x_at * LINE + y_at) * LINE + z_at) * cap
-                    parts.append(value[first : first + cap])
-        return jnp.concatenate(parts, axis=0)
-
-    def expert(e):
-        for copy in weights(e):
-            copy.wait()
-        for p in paths:
-            drain(arrived.at[pl.ds((p * 2 + e) * per_expert, 3 * group), :], fwd_recv.at[p, e])
-        row_at = pl.ds(e * per_expert, per_expert)
-        grad_at = pl.ds((2 + e) * per_expert, per_expert)
-
-        @pl.loop(0, hidden_units // f_tile)
-        def _(n):
-            units = pl.ds(pl.multiple_of(n * f_tile, f_tile), f_tile)
-            gate = jnp.dot(arrived[row_at, :], wg[:, units], preferred_element_type=F32)
-            up = jnp.dot(arrived[row_at, :], wu[:, units], preferred_element_type=F32)
-            back = lax.dot_general(arrived[grad_at, :], wd[units, :], transposed, preferred_element_type=F32)
-            back = reorder(back)
-            sigma = jax.nn.sigmoid(gate)
-            active = gate * sigma
-            hidden = (active * up).astype(BF16).astype(F32)
-            term = hidden * back
-            gg_s[:, units] = (back * up * sigma * (1.0 + gate * (1.0 - sigma))).astype(BF16)
-            ug_s[:, units] = (back * active).astype(BF16)
-            term = term[:, :128] + term[:, 128:]
-
-            @pl.when(n == 0)
-            def _():
-                score_acc[...] = term
-
-            @pl.when(n > 0)
-            def _():
-                score_acc[...] += term
-
-        for p in paths:
-
-            @pl.loop(0, cols // d_tile)
-            def _(n, p=p):
-                lanes = pl.ds(pl.multiple_of(p * cols + n * d_tile, d_tile), d_tile)
-                grad = lax.dot_general(gg_s[...], wg[lanes, :], transposed, preferred_element_type=F32)
-                grad = grad + lax.dot_general(ug_s[...], wu[lanes, :], transposed, preferred_element_type=F32)
-                blocks[pl.ds(e * per_expert, per_expert), lanes] = to_return(grad, p).astype(BF16)
-
-            for q in (1, 0):
-                for j in far_first:
-                    ret_copy(p, e, j, q).start()
-                own_return(p, e, q).start()
-
-        score = jnp.broadcast_to(jnp.sum(score_acc[...], axis=1, keepdims=True), (per_expert, 128))
-        if e == 0:
-            score_0[...] = score
-        else:
-            score_0[...] = jnp.where(low, score_0[...], score)
-
     def score_copy(j):
         return remote(
             score_s.at[wrap(y + j)], score_r.at[LINE - j], sc_send, sc_recv,
             device(ROWS, z, xh, wrap(y + j)),
         )
 
-    expert(0)
+    expert(0, 1)
     for copy in weights(1):
         copy.start()
-    expert(1)
+    for copy in weights(1):
+        copy.wait()
+    expert(1, 1)
+    expert(1, 0)
     blank = jnp.zeros((128 - slot, 128), F32)
     first = lax.broadcasted_iota(jnp.int32, (8, 128), 0) < 4
     for y_src in range(LINE):
@@ -528,6 +529,11 @@
     drain(cg_r, cg_send)
 
 
+def hand_on(grad_in, score_in, grad_out, score_out):
+    grad_out[...] = grad_in[...]
+    score_out[...] = score_in[...]
+
+
 def on_device(layer_input, out_grad, expert_ids, combine, w_gate, w_up, w_down):
     tok, width = layer_input.shape[1:]
     hidden_units = w_gate.shape[3]
@@ -535,6 +541,7 @@
     cap = 3 * tok * expert_ids.shape[2] // (2 * experts)
     slot = 2 * cap
     per_expert = LINE * LINE * slot
+    part_rows = per_expert // 2
     cols = width // 2
     vmem, hbm = pl.BlockSpec(memory_space=pltpu.VMEM), pl.BlockSpec(memory_space=pl.ANY)
     dma = pltpu.SemaphoreType.DMA
@@ -545,6 +552,7 @@
         out_specs=(vmem, vmem),
         scratch_shapes=[
             pltpu.VMEM((2 * LINE * 2 * tok, width), BF16),
+            pltpu.VMEM((part_rows, width), BF16),
             pltpu.VMEM((2 * LINE * 2, 16, tok), F32),
             pltpu.VMEM((2 * 3 * 2 * LINE * slot, width), BF16),
             pltpu.VMEM((2 * 2 * per_expert, width), BF16),
@@ -558,16 +566,16 @@
             pltpu.VMEM((width, hidden_units), BF16),
             pltpu.VMEM((width, hidden_units), BF16),
             pltpu.VMEM((hidden_units, width), BF16),
-            pltpu.VMEM((per_expert, hidden_units), BF16),
-            pltpu.VMEM((per_expert, hidden_units), BF16),
+            pltpu.VMEM((part_rows, hidden_units), BF16),
+            pltpu.VMEM((part_rows, hidden_units), BF16),
             pltpu.VMEM((per_expert, 128), F32),
             pltpu.VMEM((LINE, 8, LINE * 128), F32),
-            pltpu.VMEM((per_expert, 128), F32),
+            pltpu.VMEM((part_rows, 128), F32),
             pltpu.VMEM((LINE, 8, LINE * 128), F32),
             pltpu.VMEM((LINE * 2, 8, tok), F32),
             pltpu.VMEM((LINE * 2 - 1, 8, tok), F32),
             dma, dma((2,)), dma((2, 2, 2)), dma((2, 2, 2)), dma((2, 2)), dma, dma, dma((2,)), dma((3,)),
-            dma, dma((2, 2)), dma, dma((2, 2)), dma((2, 2)), dma, dma, dma, dma,
+            dma, dma((2, 2, 2)), dma, dma((2, 2)), dma((2, 2)), dma, dma, dma, dma,
             dma, dma((2, 2)), dma((2,)), dma((2,)), dma, dma,
         ],
         compiler_params=pltpu.CompilerParams(
@@ -578,6 +586,13 @@
         ),
         name="routed_backward",
     )(layer_input[0], out_grad[0], expert_ids[0].T, combine[0].T, w_gate[0], w_up[0], w_down[0])
+    grad, scores = pl.pallas_call(
+        hand_on,
+        out_shape=(jax.ShapeDtypeStruct((tok, width), BF16), jax.ShapeDtypeStruct((8, tok), BF16)),
+        in_specs=[vmem, vmem],
+        out_specs=(vmem, vmem),
+        name="results",
+    )(grad, scores)
     return grad[None], scores.T[None]
 
 

time: 177 us -> 170 us (0.960)
  Pallas kernels: 171 us -> 167 us
  local copies, waits for them, and re-layouts: 3.13 us -> 0 us
    pallas_call x1, Pallas kernels: 171 us -> 165 us  [on_device(): pl.pallas_call(functools.partial(kernel, tok, cap, width, hidden_units),...]
    unnamed x2 -> x0, local copies, waits for them, and re-layouts: 3.13 us -> none
    pallas_call x0 -> x1, Pallas kernels: none -> 1.87 us  [on_device(): pl.pallas_call(hand_on, out_shape=(jax.ShapeDtypeStruct((tok, width), BF1...]
where the time goes in v3:
time: 170 us; the launch traced here: 168 us
  Pallas kernels  167 us (98%)
    pallas_call x1, Pallas kernels, on_device(): pl.pallas_call(functools.partial(kernel, tok, cap, width, hidden_units),...  165 us

profile of v3, /device:TPU:0, one launch (start us, length us, event | category | flops | bytes accessed | tf_op | source)
XLA Modules:
  0.0 167.5 jit_solution(17661584875353920728)
XLA Ops:
  0.6 165.0 %routed_backward.1 = (bf16[128,2048]{1,0:T(8,128)(2,1)}, bf16[8,128]{1,0:T(8,128)(2,1)}) custom-call(bf16[128,2048]{1,0:T(8,128)(2,1)} %bitcast.18, bf16[128,2048]{1,0:T(8,128)(2,1)} %bitcast.19, s32[8,128]{1,0:T(8,128)} %bitcast.21, f32[8,128]{1,0:T(8,128)} %bitcast.22, bf16[2,2048,768]{2,1,0:T(8,128)(2,1)} %bitcast.15, bf16[2,2048,768]{2,1,0:T(8,128)(2,1)} %bitcast.16, ...), custom_call_target="tpu_custom_call" | custom-call | flops 24159191040 | bytes 25165824 | tf_op jit(solution)/shard_map/routed_backward/pallas_call | solution.py:548
  165.6 1.9 %results.1 = (bf16[128,2048]{1,0:T(8,128)(2,1)}, bf16[8,128]{1,0:T(8,128)(2,1)}) custom-call(bf16[128,2048]{1,0:T(8,128)(2,1)} %get-tuple-element.6.grad_in, bf16[8,128]{1,0:T(8,128)(2,1)} %get-tuple-element.7.score_in), custom_call_target="tpu_custom_call" | custom-call | tf_op jit(solution)/shard_map/results/pallas_call | solution.py:589

commit v4 on v3

--- a/solution.py
+++ b/solution.py
@@ -18,11 +18,11 @@
     tok, cap, width, hidden_units,
     rows_in, grads_in, ids_in, share_in, gate_w, up_w, down_w,
     out_ref, cg_ref,
-    blocks, early, metas, staged, arrived, returned, near, far, beside, final,
+    blocks, early, metas, staged, arrived, returned, near, near_own, far, beside, final,
     sel_s, wsel_s, wg, wu, wd, gg_s, ug_s, score_0, score_s, score_acc, score_r, cg_s, cg_r,
     block_send, x_recv, xn_recv, ag_recv, ag_far, meta_send, meta_recv, own_sem, w_sem,
-    fwd_send, fwd_recv, ret_send, ret_recv, ret_own, sc_send, sc_recv, cg_send, cg_recv,
-    rs_send, rs_recv, far_recv, beside_recv, fin_send, fin_recv,
+    fwd_send, fwd_recv, ret_send, ret_recv, sc_send, sc_recv, cg_send, cg_recv,
+    rs_send, rs_recv, near_recv, far_recv, beside_recv, fin_send, fin_recv,
 ):
     slot = 2 * cap
     group = LINE * slot
@@ -80,7 +80,6 @@
     barrier = pltpu.get_barrier_semaphore()
     for peer in peers:
         pl.semaphore_signal(barrier, inc=1, device_id=peer, device_id_type=MESH)
-    pl.semaphore_wait(barrier, len(peers))
 
     def own_half(p, part):
         return inputs[p].at[pl.ds(pl.multiple_of(part * half, half), half), :]
@@ -126,9 +125,24 @@
 
     others = [(i, q) for i in range(LINE) for q in range(2) if (i, q) != (0, 0)]
     paths = (ROWS, GRADS)
+    def in_weights(e):
+        return [pltpu.make_async_copy(src.at[e], dst.at[e], w_sem.at[e]) for src, dst in ((gate_w, wg), (up_w, wu))]
+
+    def out_weights(e):
+        return [pltpu.make_async_copy(down_w.at[e], wd, w_sem.at[2])]
+
+    own = []
+    for p in paths:
+        own.append(pltpu.make_async_copy(inputs[p], place(p, line[p], xh), own_sem.at[p]))
+        own[-1].start()
+
+    for copy in in_weights(0) + out_weights(0) + in_weights(1):
+        copy.start()
     for p in paths:
         metas[meta_at(p, line[p], xh), 0:8] = ids_in[...].astype(F32)
         metas[meta_at(p, line[p], xh), 8:16] = share_in[...]
+    pl.semaphore_wait(barrier, len(peers))
+    for p in paths:
         for i, q in others:
             meta_copy(p, i, q).start()
     for p in paths:
@@ -138,19 +152,10 @@
         for p in paths:
             for d in range(2):
                 ag_copy(p, 0, d, k).start()
-    own = []
-    for p in paths:
-        own.append(pltpu.make_async_copy(inputs[p], place(p, line[p], xh), own_sem.at[p]))
-        own[-1].start()
-
-    def weights(e):
-        return [
-            pltpu.make_async_copy(src.at[e], dst, w_sem.at[i])
-            for i, (src, dst) in enumerate(((gate_w, wg), (up_w, wu), (down_w, wd)))
-        ]
-
-    for copy in weights(0):
-        copy.start()
+    def wait_weights(e):
+        drain(wg, w_sem.at[e])
+        out_weights(e)[0].wait()
+
     all_metas = metas.at[pl.ds(0, 2 * len(others))]
     drain(all_metas, meta_recv)
 
@@ -249,12 +254,9 @@
 
     def ret_copy(p, e, j, q):
         return remote(
-            grads_for(p, e, q, j), returned.at[p, q, LINE - j, e], ret_send, ret_recv.at[p, q],
+            grads_for(p, e, q, j), returned.at[p, q, LINE - j - 1, e], ret_send, ret_recv.at[p, q],
             device(p, line[p], xh, wrap(cross[p] + j)),
         )
-
-    def own_return(p, e, q):
-        return pltpu.make_async_copy(grads_for(p, e, q, 0), returned.at[p, q, 0, e], ret_own.at[p, q])
 
     transposed = (((1,), (1,)), ((), ()))
     f_tile = 256
@@ -275,8 +277,8 @@
         @pl.loop(0, hidden_units // f_tile)
         def _(n):
             units = pl.ds(pl.multiple_of(n * f_tile, f_tile), f_tile)
-            gate = jnp.dot(arrived[row_at, :], wg[:, units], preferred_element_type=F32)
-            up = jnp.dot(arrived[row_at, :], wu[:, units], preferred_element_type=F32)
+            gate = jnp.dot(arrived[row_at, :], wg[e, :, units], preferred_element_type=F32)
+            up = jnp.dot(arrived[row_at, :], wu[e, :, units], preferred_element_type=F32)
             back = lax.dot_general(arrived[grad_at, :], wd[units, :], transposed, preferred_element_type=F32)
             back = turn(back)
             sigma = jax.nn.sigmoid(gate)
@@ -295,19 +297,20 @@
             def _():
                 score_acc[...] += term
 
+        if (e, q) == (0, 1):
+            out_weights(1)[0].start()
         for p in paths:
 
             @pl.loop(0, cols // d_tile)
             def _(n, p=p):
                 lanes = pl.ds(pl.multiple_of(p * cols + n * d_tile, d_tile), d_tile)
-                grad = lax.dot_general(gg_s[...], wg[lanes, :], transposed, preferred_element_type=F32)
-                grad = grad + lax.dot_general(ug_s[...], wu[lanes, :], transposed, preferred_element_type=F32)
+                grad = lax.dot_general(gg_s[...], wg[e, lanes, :], transposed, preferred_element_type=F32)
+                grad = grad + lax.dot_general(ug_s[...], wu[e, lanes, :], transposed, preferred_element_type=F32)
                 grad = (grad if p == ROWS else turn(grad)).astype(BF16)
                 grad_rows(p, e, q, part_rows, 0)[:, pl.ds(pl.multiple_of(n * d_tile, d_tile), d_tile)] = grad
 
             for j in far_first:
                 ret_copy(p, e, j, q).start()
-            own_return(p, e, q).start()
 
         score = jnp.broadcast_to(jnp.sum(score_acc[...], axis=1, keepdims=True), (part_rows, 128))
         rows = pl.ds(pl.multiple_of(offset, part_rows), part_rows)
@@ -342,8 +345,7 @@
         x_wait(p)
         for k in range(2):
             xn_copy(p, far_way[p], k).start()
-    for copy in weights(0):
-        copy.wait()
+    wait_weights(0)
     expert(0, 0)
     for p in paths:
         xn_wait(p, near_way[p], 0)
@@ -372,12 +374,81 @@
         )
 
     expert(0, 1)
-    for copy in weights(1):
-        copy.start()
-    for copy in weights(1):
-        copy.wait()
+    wait_weights(1)
     expert(1, 1)
     expert(1, 0)
+    drain(staged, fwd_send)
+
+    def partial_at(p, at, x_at, part=None, h=None):
+        start = (x_at * LINE + at) * tok
+        lanes = pl.ds(p * cols, cols) if h is None else pl.ds(p * cols + h * (cols // 2), cols // 2)
+        if part is None:
+            return staged.at[pl.ds(pl.multiple_of(start, tok), tok), lanes]
+        return staged.at[pl.ds(pl.multiple_of(start + part * half, half), half), lanes]
+
+    def combine(p, s):
+        x_at, pair_at = chunk(p, s)
+        take = pl.ds(pl.multiple_of(pair_at * slot, 16), slot)
+        parts = []
+        for e in range(2):
+            parts.append(grads_for(p, e, s // 2, 0)[take, :])
+            parts += [returned[p, s // 2, j - 1, e, take, :] for j in range(1, LINE)]
+        gathered = jnp.concatenate(parts, axis=0)
+        rows = pl.ds(pl.multiple_of((x_at * 2 + pair_at) * pair, pair), pair)
+        for n in range(cols // tile):
+            staged[rows, pl.ds(p * cols + n * tile, tile)] = jnp.dot(
+                wsel_s[p, s], gathered[:, n * tile : (n + 1) * tile], preferred_element_type=F32
+            ).astype(BF16)
+
+    def rs_copy(p, d, k, h=None):
+        step = 1 - 2 * d
+        at = wrap(line[p] + 2) if k == 0 else wrap(line[p] + step)
+        part = 1 - d if k == 1 else d
+        dst = far.at[p, d] if k == 0 else near_own.at[p, h, d, pl.ds(pl.multiple_of(part * half, half), half)]
+        return remote(
+            partial_at(p, at, xh, part, h), dst, rs_send, far_recv.at[p] if k == 0 else near_recv.at[p, h],
+            device(p, wrap(line[p] + step), xh, cross[p]),
+        )
+
+    def rs_whole(p, d):
+        step = 1 - 2 * d
+        return remote(
+            partial_at(p, wrap(line[p] + step), 1 - xh), near.at[p, d], rs_send, rs_recv.at[p],
+            device(p, wrap(line[p] + step), xh, cross[p]),
+        )
+
+    def beside_copy(p):
+        return remote(
+            partial_at(p, wrap(line[p] + 2), 1 - xh), beside.at[p], rs_send, beside_recv.at[p],
+            device(p, line[p], 1 - xh, cross[p]),
+        )
+
+    def fin_copy(p, q, h=None):
+        lanes = pl.ds(0, cols) if h is None else pl.ds(h * (cols // 2), cols // 2)
+        return remote(
+            partial_at(p, line[p], column(q), None, h), final.at[q, p, :, lanes], fin_send, fin_recv,
+            device(p, line[p], column(q), cross[p], before),
+        )
+
+    def cg_copy(i, q):
+        return remote(
+            cg_s.at[2 * i + q], cg_r.at[2 * i + q - 1], cg_send, cg_recv,
+            device(ROWS, member(ROWS, i), column(q), y),
+        )
+
+    def sum_up(mine, others):
+        mine[...] = (mine[...].astype(F32) + others[0].astype(F32) + others[1].astype(F32)).astype(BF16)
+
+    def wait_returned(p, q):
+        drain(returned.at[p, q], ret_recv.at[p, q])
+
+    for p in paths:
+        wait_returned(p, 1)
+        combine(p, 3)
+        beside_copy(p).start()
+        rs_whole(p, near_way[p]).start()
+        combine(p, 2)
+        rs_whole(p, far_way[p]).start()
     blank = jnp.zeros((128 - slot, 128), F32)
     first = lax.broadcasted_iota(jnp.int32, (8, 128), 0) < 4
     for y_src in range(LINE):
@@ -388,99 +459,31 @@
     for j in far_first:
         score_copy(j).start()
     score_r[0] = score_s[y]
-    drain(staged, fwd_send)
-
-    def partial_at(p, at, x_at, part=None):
-        start = (x_at * LINE + at) * tok
-        lanes = pl.ds(p * cols, cols)
-        if part is None:
-            return staged.at[pl.ds(pl.multiple_of(start, tok), tok), lanes]
-        return staged.at[pl.ds(pl.multiple_of(start + part * half, half), half), lanes]
-
-    def combine(p, s):
-        x_at, pair_at = chunk(p, s)
-        take = pl.ds(pl.multiple_of(pair_at * slot, 16), slot)
-        gathered = jnp.concatenate([returned[p, s // 2, j, e, take, :] for e in range(2) for j in range(LINE)], axis=0)
-        rows = pl.ds(pl.multiple_of((x_at * 2 + pair_at) * pair, pair), pair)
-        for n in range(cols // tile):
-            staged[rows, pl.ds(p * cols + n * tile, tile)] = jnp.dot(
-                wsel_s[p, s], gathered[:, n * tile : (n + 1) * tile], preferred_element_type=F32
-            ).astype(BF16)
-
-    def rs_copy(p, d, k):
-        step = 1 - 2 * d
-        at = wrap(line[p] + 2) if k == 0 else wrap(line[p] + step)
-        part = 1 - d if k == 1 else d
-        dst = far.at[p, d] if k == 0 else near.at[p, 0, d, pl.ds(pl.multiple_of(part * half, half), half)]
-        return remote(
-            partial_at(p, at, xh, part), dst, rs_send, far_recv.at[p] if k == 0 else rs_recv.at[p, 0],
-            device(p, wrap(line[p] + step), xh, cross[p]),
-        )
-
-    def rs_whole(p, d):
-        step = 1 - 2 * d
-        return remote(
-            partial_at(p, wrap(line[p] + step), 1 - xh), near.at[p, 1, d], rs_send, rs_recv.at[p, 1],
-            device(p, wrap(line[p] + step), xh, cross[p]),
-        )
-
-    def beside_copy(p):
-        return remote(
-            partial_at(p, wrap(line[p] + 2), 1 - xh), beside.at[p], rs_send, beside_recv.at[p],
-            device(p, line[p], 1 - xh, cross[p]),
-        )
-
-    def fin_copy(p, q):
-        x_at = xh if q == 0 else 1 - xh
-        return remote(
-            partial_at(p, line[p], x_at), final.at[q, p], fin_send, fin_recv,
-            device(p, line[p], x_at, cross[p], before),
-        )
-
-    def cg_copy(i, q):
-        return remote(
-            cg_s.at[2 * i + q], cg_r.at[2 * i + q - 1], cg_send, cg_recv,
-            device(ROWS, member(ROWS, i), column(q), y),
-        )
-
-    def sum_up(p, q):
-        mine = partial_at(p, line[p], column(q))
-        mine[...] = (
-            mine[...].astype(F32) + near[p, q, 0].astype(F32) + near[p, q, 1].astype(F32)
-        ).astype(BF16)
-
-    def wait_returned(p, q):
-        drain(returned.at[p, q, pl.ds(1, 3)], ret_recv.at[p, q])
-        drain(returned.at[p, q, 0], ret_own.at[p, q])
-
-    for p in paths:
-        wait_returned(p, 1)
-        combine(p, 3)
-        beside_copy(p).start()
-        rs_whole(p, near_way[p]).start()
-        combine(p, 2)
-        rs_whole(p, far_way[p]).start()
     for p in paths:
         wait_returned(p, 0)
         combine(p, 1)
-        rs_copy(p, near_way[p], 1).start()
+    for p in paths:
         drain(beside.at[p], beside_recv.at[p])
         mine = partial_at(p, wrap(line[p] + 2), xh)
         mine[...] = (mine[...].astype(F32) + beside[p].astype(F32)).astype(BF16)
         for d in range(2):
             rs_copy(p, d, 0).start()
+        for h in range(2):
+            rs_copy(p, near_way[p], 1, h).start()
+    for p in paths:
         combine(p, 0)
-        rs_copy(p, far_way[p], 1).start()
-    for p in paths:
-        drain(near.at[p, 1], rs_recv.at[p, 1])
-        sum_up(p, 1)
+        for h in range(2):
+            rs_copy(p, far_way[p], 1, h).start()
+    for p in paths:
+        drain(near.at[p], rs_recv.at[p])
+        sum_up(partial_at(p, line[p], 1 - xh), near[p])
         fin_copy(p, 1).start()
 
     drain(score_r.at[pl.ds(1, 3)], sc_recv)
     row = lax.broadcasted_iota(jnp.int32, (8, 128), 0)
     numbers = expert_numbers(ROWS).astype(F32)
     pad = jnp.zeros((128 - slot, pair), BF16)
-    for s in chunks:
+    def score_chunk(s):
         x_at, pair_at = chunk(ROWS, s)
         take = pl.ds(pl.multiple_of((x_at * 2 + pair_at) * 128, 128), 128)
         by_expert = jnp.zeros((8, pair), F32)
@@ -502,16 +505,24 @@
             if (i, q) != (0, 0):
                 cg_copy(i, q).start()
 
+    for s in (0, 1):
+        score_chunk(s)
     for p in paths:
         drain(far.at[p], far_recv.at[p])
         for d in range(2):
             mid = partial_at(p, wrap(line[p] + 1 - 2 * d), xh, d)
             mid[...] = (mid[...].astype(F32) + far[p, d].astype(F32)).astype(BF16)
-            rs_copy(p, d, 2).start()
-    for p in paths:
-        drain(near.at[p, 0], rs_recv.at[p, 0])
-        sum_up(p, 0)
-        fin_copy(p, 0).start()
+            rs_copy(p, d, 2, 0).start()
+    for p in paths:
+        for d in range(2):
+            rs_copy(p, d, 2, 1).start()
+    for s in (2, 3):
+        score_chunk(s)
+    for h in range(2):
+        for p in paths:
+            drain(near_own.at[p, h], near_recv.at[p, h])
+            sum_up(partial_at(p, line[p], xh, None, h), near_own[p, h])
+            fin_copy(p, 0, h).start()
 
     drain(cg_r, cg_recv)
     total = cg_s[0]
@@ -556,15 +567,16 @@
             pltpu.VMEM((2 * LINE * 2, 16, tok), F32),
             pltpu.VMEM((2 * 3 * 2 * LINE * slot, width), BF16),
             pltpu.VMEM((2 * 2 * per_expert, width), BF16),
-            pltpu.VMEM((2, 2, LINE, 2, 2 * slot, cols), BF16),
-            pltpu.VMEM((2, 2, 2, tok, cols), BF16),
+            pltpu.VMEM((2, 2, LINE - 1, 2, 2 * slot, cols), BF16),
+            pltpu.VMEM((2, 2, tok, cols), BF16),
+            pltpu.VMEM((2, 2, 2, tok, cols // 2), BF16),
             pltpu.VMEM((2, 2, tok // 2, cols), BF16),
             pltpu.VMEM((2, tok, cols), BF16),
             pltpu.VMEM((2, 2, tok, cols), BF16),
             pltpu.VMEM((2, LINE, 8 * slot, 2 * tok), BF16),
             pltpu.VMEM((2, LINE, 2 * tok, 8 * slot), BF16),
-            pltpu.VMEM((width, hidden_units), BF16),
-            pltpu.VMEM((width, hidden_units), BF16),
+            pltpu.VMEM((2, width, hidden_units), BF16),
+            pltpu.VMEM((2, width, hidden_units), BF16),
             pltpu.VMEM((hidden_units, width), BF16),
             pltpu.VMEM((part_rows, hidden_units), BF16),
             pltpu.VMEM((part_rows, hidden_units), BF16),
@@ -575,8 +587,8 @@
             pltpu.VMEM((LINE * 2, 8, tok), F32),
             pltpu.VMEM((LINE * 2 - 1, 8, tok), F32),
             dma, dma((2,)), dma((2, 2, 2)), dma((2, 2, 2)), dma((2, 2)), dma, dma, dma((2,)), dma((3,)),
-            dma, dma((2, 2, 2)), dma, dma((2, 2)), dma((2, 2)), dma, dma, dma, dma,
-            dma, dma((2, 2)), dma((2,)), dma((2,)), dma, dma,
+            dma, dma((2, 2, 2)), dma, dma((2, 2)), dma, dma, dma, dma,
+            dma, dma((2,)), dma((2, 2)), dma((2,)), dma((2,)), dma, dma,
         ],
         compiler_params=pltpu.CompilerParams(
             collective_id=0, has_side_effects=True, vmem_limit_bytes=63 << 20

time: 170 us -> 168 us (0.988)
  Pallas kernels: 167 us -> 165 us
where the time goes in v4:
time: 168 us; the launch traced here: 166 us
  Pallas kernels  165 us (98%)
    pallas_call x1, Pallas kernels, on_device(): pl.pallas_call(functools.partial(kernel, tok, cap, width, hidden_units),...  163 us

profile of v4, /device:TPU:0, one launch (start us, length us, event | category | flops | bytes accessed | tf_op | source)
XLA Modules:
  0.0 165.9 jit_solution(9702579864386994478)
XLA Ops:
  0.6 163.4 %routed_backward.1 = (bf16[128,2048]{1,0:T(8,128)(2,1)}, bf16[8,128]{1,0:T(8,128)(2,1)}) custom-call(bf16[128,2048]{1,0:T(8,128)(2,1)} %bitcast.18, bf16[128,2048]{1,0:T(8,128)(2,1)} %bitcast.19, s32[8,128]{1,0:T(8,128)} %bitcast.21, f32[8,128]{1,0:T(8,128)} %bitcast.22, bf16[2,2048,768]{2,1,0:T(8,128)(2,1)} %bitcast.15, bf16[2,2048,768]{2,1,0:T(8,128)(2,1)} %bitcast.16, ...), custom_call_target="tpu_custom_call" | custom-call | flops 24159191040 | bytes 25165824 | tf_op jit(solution)/shard_map/routed_backward/pallas_call | solution.py:559
  164.0 1.9 %results.1 = (bf16[128,2048]{1,0:T(8,128)(2,1)}, bf16[8,128]{1,0:T(8,128)(2,1)}) custom-call(bf16[128,2048]{1,0:T(8,128)(2,1)} %get-tuple-element.6.grad_in, bf16[8,128]{1,0:T(8,128)(2,1)} %get-tuple-element.7.score_in), custom_call_target="tpu_custom_call" | custom-call | tf_op jit(solution)/shard_map/results/pallas_call | solution.py:601
